TPU v7x, 128 devices: a whole 4x4x4 slice. The times are simulated.
128 devices in a mesh: dp: 16 (over z, y), mp: 8 (over x, core).
Axes of the slice: x: 4, y: 4, z: 4, core: 2. Of those that a mesh axis runs over, the one named last changes fastest.
Arguments:
- hidden: bfloat16 [256, 5120], P('dp', 'mp'), may hold values from -6 to 6
- w_query: bfloat16 [5120, 8192], P(None, 'mp'), may hold values from -0.078125 to 0.078125
- w_key: bfloat16 [5120, 1024], P(None, 'mp'), may hold values from -0.078125 to 0.078125
- w_value: bfloat16 [5120, 1024], P(None, 'mp'), may hold values from -0.078125 to 0.078125
- query_gain: float32 [128], replicated, may hold values from 0.5 to 3
- key_gain: float32 [128], replicated, may hold values from 0.5 to 3
- kv_pool: bfloat16 [12288, 16, 8, 256], P('dp', None, 'mp')
- page_table: int32 [256, 48], replicated, may hold values from 0 to 767, as said below
- parent: int32 [256], replicated, may hold values from 0 to 255, as said below
- surviving: int32 [256], replicated, may hold values from 0 to 1, as said below
Outputs:
- refilled_pool: bfloat16 [12288, 16, 8, 256], P('dp', None, 'mp')
- attention: bfloat16 [256, 8192], P('dp', 'mp')
Inputs may be any that keep to these rules, and one draw needn't show every extreme that they name: `page_table`: for each group, its 16 rows together name each page 0 to 767 once. A pruned branch's parent survives. For every group, at most 2 of its pruned branches have parents in any one group, and this is reached in every draw; those branches have different parents. For a surviving branch the entry names some surviving branch and is not used. `surviving`: each group keeps 2 to 4 of its branches.
All inputs are finite; a program needn't handle non-finite values.
Results may differ from a plain program's by a relative error of at most 0.015.
The roundings to bfloat16 on the way count: a program that leaves them out, or rounds other values in their place, can miss the bound.
Values may be sent and summed in bfloat16 or wider, within the bound.
A program may use at most 128 MiB of HBM per device.

v0:
```python
import math

import jax
import jax.numpy as jnp
from jax import lax
from jax.sharding import PartitionSpec as P

H = 64
KVH = 8
HD = 128
PAGE = 16
NPAGE = 48
CAP = 2


def normalize(values, gain):
    return values * lax.rsqrt(jnp.mean(values * values, -1, keepdims=True) + 1e-06) * gain


def attend_sets(query_rows, key_rows, value_rows, token_sets):
    own_score = jnp.einsum(
        "nkgd,nkd->nkg", query_rows, key_rows, preferred_element_type=jnp.float32
    )
    score_list = []
    peak_score = own_score
    for tokens, allowed in token_sets:
        scores = jnp.einsum(
            "nkgd,tkd->nkgt", query_rows, tokens[..., :HD], preferred_element_type=jnp.float32
        )
        scores = jnp.where(allowed[:, None, None, :], scores, -jnp.inf)
        score_list.append(scores)
        peak_score = jnp.maximum(peak_score, jnp.max(scores, -1))
    own_term = jnp.exp(own_score - peak_score)
    total_mass = own_term
    term_list = []
    for scores in score_list:
        expo_terms = jnp.exp(scores - peak_score[..., None])
        term_list.append(expo_terms)
        total_mass = total_mass + jnp.sum(expo_terms, -1)
    own_weight = (own_term / total_mass).astype(jnp.bfloat16)
    mixed_out = (
        own_weight.astype(jnp.float32)[..., None] * value_rows.astype(jnp.float32)[:, :, None, :]
    )
    for expo_terms, (tokens, allowed) in zip(term_list, token_sets):
        weights = (expo_terms / total_mass[..., None]).astype(jnp.bfloat16)
        mixed_out = mixed_out + jnp.einsum(
            "nkgt,tkd->nkgd", weights, tokens[..., HD:], preferred_element_type=jnp.float32
        )
    return mixed_out.astype(jnp.bfloat16)


def shards(
    hidden, w_query, w_key, w_value, query_gain, key_gain, kv_pool, page_table, parent, surviving
):
    features = lax.all_gather(hidden, "mp", axis=1, tiled=True)
    branch_count = features.shape[0]
    kv_local = kv_pool.shape[2]
    pool_pages = kv_pool.shape[0]
    head_group = H // KVH
    groups_dp = lax.axis_size("dp")
    my_group = lax.axis_index("dp")
    query_full = jnp.dot(features, w_query, preferred_element_type=jnp.float32).reshape(
        branch_count, kv_local, head_group, HD
    )
    query_rows = (normalize(query_full, query_gain) / math.sqrt(HD)).astype(jnp.bfloat16)
    key_full = jnp.dot(features, w_key, preferred_element_type=jnp.float32).reshape(
        branch_count, kv_local, HD
    )
    key_rows = normalize(key_full, key_gain).astype(jnp.bfloat16)
    value_rows = (
        jnp.dot(features, w_value, preferred_element_type=jnp.float32)
        .reshape(branch_count, kv_local, HD)
        .astype(jnp.bfloat16)
    )
    total_branches = parent.shape[0]
    slot_ids = jnp.arange(total_branches, dtype=jnp.int32)
    child_mask = surviving == 0
    source_group = parent // branch_count
    target_group = slot_ids // branch_count
    earlier = (target_group[:, None] == target_group[None, :]) & (
        source_group[:, None] == source_group[None, :]
    )
    earlier = earlier & child_mask[None, :] & (slot_ids[None, :] < slot_ids[:, None])
    child_rank = jnp.sum(earlier.astype(jnp.int32), axis=1)
    group_ids = jnp.arange(groups_dp, dtype=jnp.int32)
    cap_ids = jnp.arange(CAP, dtype=jnp.int32)
    served = child_mask & (source_group == my_group)
    outgoing = (
        (target_group[None, None, :] == group_ids[:, None, None])
        & (child_rank[None, None, :] == cap_ids[None, :, None])
        & served[None, None, :]
    )
    parent_slot = jnp.sum(jnp.where(outgoing, parent[None, None, :], 0), axis=2)
    packed = kv_pool[page_table[parent_slot]]
    arrived = lax.all_to_all(packed, "dp", split_axis=0, concat_axis=0, tiled=True)
    first_slot = my_group * branch_count
    my_table = lax.dynamic_slice_in_dim(page_table, first_slot, branch_count, 0)
    my_child = lax.dynamic_slice_in_dim(child_mask, first_slot, branch_count, 0)
    my_source = lax.dynamic_slice_in_dim(source_group, first_slot, branch_count, 0)
    my_rank = jnp.minimum(
        lax.dynamic_slice_in_dim(child_rank, first_slot, branch_count, 0), CAP - 1
    )
    page_ids = jnp.arange(pool_pages, dtype=jnp.int32)
    entry_ids = jnp.arange(my_table.size, dtype=jnp.int32)
    owner_match = my_table.reshape(-1)[None, :] == page_ids[:, None]
    owner_entry = jnp.sum(jnp.where(owner_match, entry_ids[None, :], 0), axis=1)
    owner_branch = owner_entry // NPAGE
    owner_position = owner_entry % NPAGE
    local_ids = jnp.arange(branch_count, dtype=jnp.int32)
    owner_onehot = owner_branch[:, None] == local_ids[None, :]
    owner_child = jnp.any(owner_onehot & my_child[None, :], axis=1)
    branch_slot = my_source * CAP + my_rank
    owner_slot = jnp.sum(jnp.where(owner_onehot, branch_slot[None, :], 0), axis=1)
    arrived_pages = arrived.reshape((-1,) + kv_pool.shape[1:])
    moved_pages = arrived_pages[owner_slot * NPAGE + owner_position]
    refilled = jnp.where(owner_child[:, None, None, None], moved_pages, kv_pool)
    pool_tokens = kv_pool.reshape(pool_pages * PAGE, kv_local, 2 * HD)
    token_owner = jnp.repeat(owner_branch, PAGE)
    pool_allowed = (token_owner[None, :] == local_ids[:, None]) & jnp.logical_not(my_child)[:, None]
    arrived_tokens = arrived.reshape(-1, kv_local, 2 * HD)
    token_slot = jnp.arange(arrived_tokens.shape[0], dtype=jnp.int32) // (NPAGE * PAGE)
    arrived_allowed = (token_slot[None, :] == branch_slot[:, None]) & my_child[:, None]
    attention = attend_sets(
        query_rows,
        key_rows,
        value_rows,
        [(pool_tokens, pool_allowed), (arrived_tokens, arrived_allowed)],
    )
    return (refilled, attention.reshape(branch_count, -1))


def solution(mesh):
    return jax.shard_map(
        shards,
        mesh=mesh,
        in_specs=(
            P("dp", "mp"),
            P(None, "mp"),
            P(None, "mp"),
            P(None, "mp"),
            P(),
            P(),
            P("dp", None, "mp", None),
            P(),
            P(),
            P(),
        ),
        out_specs=(P("dp", None, "mp", None), P("dp", "mp")),
        check_vma=False,
    )
```

profile of v0, /device:TPU:1, one launch (start us, length us, event | category | flops | bytes accessed | tf_op | source)
XLA Modules:
  0.0 265.1 jit_solution(3444531407735201098)
XLA Ops:
  0.7 0.8 compare_and_fusion.1
  1.5 0.2 convert_reduce_fusion
  1.7 0.8 select_reduce_fusion.2
  2.6 0.1 reshape.434
  2.7 0.9 copy.44
  3.6 0.6 gather_fusion
  4.3 9.6 %gather_fusion.1 = bf16[1536,16,256]{2,1,0:T(8,128)(2,1)} fusion(bf16[768,16,256]{2,1,0:T(8,128)(2,1)} %bitcast.142, s32[2048]{0:T(1024)S(1)} %pad_clamp_fusion), kind=kCustom, calls=%fused_computation.1 | custom fusion | bytes 25171968 | tf_op jit(solution)/shard_map/gather | solution.py:94
  13.9 8.8 %all-to-all-start = ((bf16[16,2,48,16,1,256]{5,3,2,1,4,0:T(8,128)(2,1)}), bf16[16,2,48,16,1,256]{5,3,2,1,4,0:T(8,128)(2,1)}, u32[]{:S(2)}, u32[]{:S(2)}) async-start(bf16[16,2,48,16,1,256]{5,3,2,1,4,0:T(8,128)(2,1)} %bitcast.147), calls=%async_computation | async-start | bytes 25165824 | tf_op jit(solution)/shard_map/all_to_all | solution.py:95
  22.7 13.9 %all_gather.3 = bf16[16,5120]{1,0:T(8,128)(2,1)S(1)} all-gather(bf16[16,640]{1,0:T(8,128)(2,1)S(1)} %copy-done.4), channel_id=1, replica_groups=mesh['dp'=16,'mp'=8] {'mp'}, dimensions={1}, use_global_device_ids=true | all-gather | bytes 184320 | tf_op jit(solution)/shard_map/all_gather | solution.py:55
  36.7 5.6 %fusion.50 = f32[16,1024]{1,0:T(8,128)S(1)} fusion(bf16[16,5120]{1,0:T(8,128)(2,1)S(1)} %all_gather.3, bf16[5120,1024]{1,0:T(8,128)(2,1)} %param.11), kind=kOutput, calls=%fused_computation.106 | convolution fusion | flops 167772160 | bytes 10715136 | tf_op jit(solution)/shard_map/dot_general | solution.py:62
  42.5 0.3 select_reduce_fusion
  42.9 0.2 eq.144
  43.1 0.2 eq.163
  43.6 0.3 select_reduce_fusion.1
  44.0 0.3 fusion.27
  44.3 0.4 multiply_reduce_fusion
  44.8 0.1 fusion.37
  44.9 0.1 fusion.40
  45.0 0.3 fusion.24
  45.4 0.2 fusion.25
  45.6 5.7 %fusion.49 = (f32[16,8]{1,0:T(8,128)S(1)}, f32[16,1,8,12288]{3,2,0,1:T(8,128)}) fusion(bf16[16,8,128]{2,1,0:T(8,128)(2,1)S(1)} %bitcast.152, bf16[12288,1,256]{2,0,1:T(8,128)(2,1)} %bitcast.143, pred[16,12288]{1,0:T(8,128)(4,1)S(1)} %fusion.25), kind=kOutput, calls=%fused_computation.105 | convolution fusion | flops 405798784 | bytes 9667072 | tf_op jit(solution)/shard_map/nkgd,tkd->nkgt/dot_general | solution.py:27
  51.3 0.3 compare_and_fusion
  51.6 157.1 %all-to-all-done = bf16[16,2,48,16,1,256]{5,3,2,1,4,0:T(8,128)(2,1)} async-done(((bf16[16,2,48,16,1,256]{5,3,2,1,4,0:T(8,128)(2,1)}), bf16[16,2,48,16,1,256]{5,3,2,1,4,0:T(8,128)(2,1)}, u32[]{:S(2)}, u32[]{:S(2)}) %all-to-all-start) | async-done | bytes 12582944 | tf_op jit(solution)/shard_map/all_to_all | solution.py:95
  208.7 9.1 %fusion.48 = (f32[16,8]{0,1:T(8,128)S(1)}, f32[16,1,8,24576]{3,0,2,1:T(8,128)}) fusion(bf16[24576,1,256]{2,0,1:T(8,128)(2,1)} %bitcast.16, pred[16,24576]{1,0:T(8,128)(4,1)S(1)} %compare_and_fusion, f32[1024]{0:T(1024)S(1)} %broadcast_bitcast_fusion, f32[16,1024]{1,0:T(8,128)S(1)} %fusion.50, f32[2,8,8,128]{3,2,1,0:T(8,128)S(1)} %bitcast.151), kind=kOutput, calls=%fused_computation.104 | convolution fusion | flops 811663232 | bytes 19403264 | tf_op jit(solution)/shard_map/nkgd,tkd->nkgt/dot_general | solution.py:27
  217.9 6.4 %fusion.2 = f32[16,8]{0,1:T(8,128)S(1)} fusion(f32[16,1,8,24576]{3,0,2,1:T(8,128)} %get-tuple-element.14, f32[16,8]{0,1:T(8,128)S(1)} %copy.47), kind=kLoop, calls=%fused_computation.9 | loop fusion | flops 6291328 | bytes 12583936 | tf_op jit(solution)/shard_map/reduce_sum | solution.py:39
  224.4 3.9 %fusion.6 = f32[16,8]{1,0:T(8,128)S(1)} fusion(f32[16,1,8,12288]{3,2,0,1:T(8,128)} %get-tuple-element.16, f32[16,8]{1,0:T(8,128)S(1)} %maximum_maximum_fusion), kind=kLoop, calls=%fused_computation.18 | loop fusion | flops 3145600 | bytes 6292480 | tf_op jit(solution)/shard_map/reduce_sum | solution.py:39
  228.4 6.4 %fusion.5 = bf16[16,8,24576]{2,0,1:T(8,128)(2,1)S(1)} fusion(f32[16,8]{0,1:T(8,128)S(1)} %copy.49, f32[16,1,8,24576]{3,0,2,1:T(8,128)} %get-tuple-element.14, f32[16,8]{0,1:T(8,128)S(1)} %copy.47), kind=kLoop, calls=%fused_computation.17 | loop fusion | flops 9437184 | bytes 18875392 | tf_op jit(solution)/shard_map/reshape.39
  234.8 4.0 %fusion.18 = f32[16,1,8,128]{3,2,0,1:T(8,128)S(1)} fusion(bf16[12288,1,256]{2,0,1:T(8,128)(2,1)S(1)} %bitcast.146, f32[16,8]{1,0:T(8,128)S(1)} %get-tuple-element.3, f32[16,1,8,12288]{3,2,0,1:T(8,128)} %get-tuple-element.16, f32[16,8]{1,0:T(8,128)S(1)} %maximum_maximum_fusion, f32[16,128]{1,0:T(8,128)S(1)} %fusion.24, f32[16,8]{1,0:T(8,128)S(1)} %get-tuple-element.2), kind=kOutput, calls=%fused_computation.29 | convolution fusion | flops 407404544 | bytes 9535488 | tf_op jit(solution)/shard_map/nkgt,tkd->nkgd/dot_general | solution.py:46
  238.9 6.6 %fusion.21 = bf16[16,1,8,128]{3,2,0,1:T(8,128)(2,1)S(1)} fusion(f32[16,1,8,128]{3,2,0,1:T(8,128)S(1)} %fusion.18, bf16[16,8,24576]{2,0,1:T(8,128)(2,1)S(1)} %fusion.5, bf16[24576,1,256]{2,0,1:T(8,128)(2,1)} %bitcast.16), kind=kOutput, calls=%fused_computation.30 | convolution fusion | flops 805339136 | bytes 12681216 | tf_op jit(solution)/shard_map/nkgt,tkd->nkgd/dot_general | solution.py:46
  245.5 0.6 copy.85
  246.1 9.7 %gather_fusion.2 = bf16[768,16,256]{2,1,0:T(8,128)(2,1)} fusion(bf16[1536,16,256]{2,1,0:T(8,128)(2,1)} %bitcast.4, s32[1024]{0:T(1024)S(1)} %pad_clamp_fusion.1), kind=kCustom, calls=%fused_computation.2 | custom fusion | bytes 12585984 | tf_op jit(solution)/shard_map/gather | solution.py:115
  255.8 9.2 %bitcast_select_fusion = bf16[768,16,1,256]{3,1,2,0:T(8,128)(2,1)} fusion(bf16[768,16,1,256]{3,1,2,0:T(8,128)(2,1)} %param.16, bf16[768,16,256]{2,1,0:T(8,128)(2,1)} %gather_fusion.2, pred[768]{0:T(1024)(128)(4,1)S(1)} %fusion.27), kind=kLoop, calls=%fused_computation.13 | loop fusion | flops 3145728 | bytes 18875136 | tf_op jit(solution)/shard_map/jit(_where)/select_n | solution.py:116
  (55 shorter events, 1.3 us)
Async XLA Ops:
  0.6 43.7 %copy-start = (bf16[5120,128]{1,0:T(8,128)(2,1)S(1)}, bf16[5120,128]{1,0:T(8,128)(2,1)}, u32[]{:S(2)}) copy-start(bf16[5120,128]{1,0:T(8,128)(2,1)} %param.12) | copy-start | bytes 3932164
  13.9 8.8 %copy-start.4 = (bf16[16,640]{1,0:T(8,128)(2,1)S(1)}, bf16[16,640]{1,0:T(8,128)(2,1)}, u32[]{:S(2)}) copy-start(bf16[16,640]{1,0:T(8,128)(2,1)} %param.10) | copy-start | bytes 61444
  13.9 194.7 %all-to-all-start = ((bf16[16,2,48,16,1,256]{5,3,2,1,4,0:T(8,128)(2,1)}), bf16[16,2,48,16,1,256]{5,3,2,1,4,0:T(8,128)(2,1)}, u32[]{:S(2)}, u32[]{:S(2)}) async-start(bf16[16,2,48,16,1,256]{5,3,2,1,4,0:T(8,128)(2,1)} %bitcast.147), calls=%async_computation | async-start | bytes 25165824 | tf_op jit(solution)/shard_map/all_to_all | solution.py:95
  36.7 5.6 %copy-start.3 = (s32[256,48]{0,1:T(8,128)S(1)}, s32[256,48]{0,1:T(8,128)}, u32[]{:S(2)}) copy-start(s32[256,48]{0,1:T(8,128)} %param.17) | copy-start | bytes 147460
  36.7 6.6 %copy-start.5 = (f32[128]{0:T(128)S(1)}, f32[128]{0:T(128)}, u32[]{:S(2)}) copy-start(f32[128]{0:T(128)} %param.14) | copy-start | bytes 1540
  36.7 8.0 %copy-start.6 = (f32[128]{0:T(128)S(1)}, f32[128]{0:T(128)}, u32[]{:S(2)}) copy-start(f32[128]{0:T(128)} %param.15) | copy-start | bytes 1540
  36.7 8.4 %copy-start.2 = (bf16[5120,128]{1,0:T(8,128)(2,1)S(1)}, bf16[5120,128]{1,0:T(8,128)(2,1)}, u32[]{:S(2)}) copy-start(bf16[5120,128]{1,0:T(8,128)(2,1)} %param.13) | copy-start | bytes 3932164
  224.4 10.4 %slice-start = ((s8[6291456]{0:T(1024)(128)(4,1)}), s8[2097152]{0:T(1024)(128)(4,1)S(1)}, s32[]{:S(2)}) async-start(s8[6291456]{0:T(1024)(128)(4,1)} %bitcast.144), calls=%async_computation.1 | async-start | bytes 4194304
  228.4 6.4 %slice-start.1 = ((s8[6291456]{0:T(1024)(128)(4,1)}), s8[4194304]{0:T(1024)(128)(4,1)S(1)}, s32[]{:S(2)}) async-start(s8[6291456]{0:T(1024)(128)(4,1)} %bitcast.144), calls=%async_computation.2 | async-start | bytes 8388608
  246.1 18.9 %copy-start.1 = (bf16[5120,128]{1,0:T(8,128)(2,1)S(1)}, bf16[5120,128]{1,0:T(8,128)(2,1)}, u32[]{:S(2)}) copy-start(bf16[5120,128]{1,0:T(8,128)(2,1)} %param.12) | copy-start | bytes 3932164
where the time goes:
time: 266 us; the launch traced here: 265 us
  waiting for transfers between devices  157 us (59%)
  matrix products  31.8 us (12%)
  other arithmetic  29.8 us (11%)
  local copies, waits for them, and re-layouts  22.7 us (9%)
  blocking collectives  13.9 us (5%)
  starting transfers between devices  8.77 us (3%)
    all_to_all x1, waiting for transfers between devices, shards(): lax.all_to_all(packed, 'dp', split_axis=0, concat_axis=0, tiled=True)  157 us
    dot_general x2, matrix products, attend_sets(): jnp.einsum('nkgd,tkd->nkgt', query_rows, tokens[..., :HD], preferred_elem...  14.8 us
    all_gather x1, blocking collectives, shards(): features = lax.all_gather(hidden, 'mp', axis=1, tiled=True)  13.9 us
    dot_general x2, matrix products, attend_sets(): jnp.einsum('nkgt,tkd->nkgd', weights, tokens[..., HD:], preferred_element...  10.7 us
    reduce_sum x2, other arithmetic, attend_sets(): total_mass = total_mass + jnp.sum(expo_terms, -1)  10.4 us
    gather x2, local copies, waits for them, and re-layouts, shards(): packed = kv_pool[page_table[parent_slot]]  10.2 us
    gather x1, local copies, waits for them, and re-layouts, shards(): moved_pages = arrived_pages[owner_slot * NPAGE + owner_position]  9.73 us
    select_n x1, other arithmetic, shards(): refilled = jnp.where(owner_child[:, None, None, None], moved_pages, kv_pool)  9.21 us
  transfers between devices with their start and end apart: 1, of which 1 were waited for; matrix products, arithmetic and copies ran while one was open for 6% of the time, Pallas kernels for 0%

commit v1 on v0

v1 whole, which is shorter than its diff:
```python
import math

import jax
import jax.numpy as jnp
from jax import lax
from jax.experimental import pallas as pl
from jax.experimental.pallas import tpu as pltpu
from jax.sharding import PartitionSpec as P

H = 64
KVH = 8
HD = 128
PAGE = 16
NPAGE = 48
BR = 16
GROUPS = 16
ALIVE = 4
KIDS = 14
SIDE = 4
NQ = 3
PQ = 2
PIECE = NQ * PQ
HALF = NPAGE // 2
MP = 8
MESH = pl.DeviceIdType.MESH
SLOTS = ALIVE + KIDS
CHUNK_TOKENS = SIDE * PQ * PAGE


def relay_kernel(
    hidden_ref, query_gain_ref, key_gain_ref, w_query_ref, w_key_ref, w_value_ref, pool_ref,
    table_ref, parent_ref, surviving_ref,
    arrived_out_ref, attention_ref,
    *scratch,
):
    scratch = list(scratch)
    gathered = [[scratch.pop(0) for _ in range(NQ)] for _ in range(2)]
    (outgoing, arrived, pool, features, w_query, w_key, w_value, project, queries, keys, values,
     peak, mass, mixed, result,
     alive_table, rank_table, source_table, child_table, slot_table,
     send_sem, recv_sem, feature_send, feature_recv, pool_sem, weight_sem, out_sem) = scratch

    group = lax.axis_index("dp")
    part = lax.axis_index("mp")
    z, y = group // SIDE, group % SIDE
    along = [z, y]
    across = [y, z]

    def device(half, gather_at, spread_at):
        if half == 0:
            return (gather_at * SIDE + spread_at, part)
        return (spread_at * SIDE + gather_at, part)

    def shifted(value, step, size=SIDE):
        return (value + step + size) % size

    pool_copy = pltpu.make_async_copy(pool_ref, pool, pool_sem)
    pool_copy.start()

    barrier = pltpu.get_barrier_semaphore()
    for step in range(1, SIDE):
        pl.semaphore_signal(barrier, inc=1, device_id=device(0, z, shifted(y, step)), device_id_type=MESH)
        pl.semaphore_signal(barrier, inc=1, device_id=device(1, y, shifted(z, step)), device_id_type=MESH)
    for step in range(1, MP):
        pl.semaphore_signal(barrier, inc=1, device_id=(group, shifted(part, step, MP)), device_id_type=MESH)

    def rank_group(at, carry):
        found = [jnp.int32(99) for _ in range(ALIVE)]
        count = jnp.int32(0)
        for branch in range(BR):
            lives = surviving_ref[at * BR + branch]
            rank_table[at * BR + branch] = count
            for k in range(ALIVE):
                found[k] = jnp.where((lives > 0) & (count == k), jnp.int32(branch), found[k])
            count = count + lives
        for k in range(ALIVE):
            alive_table[at * ALIVE + k] = found[k]
        return carry

    lax.fori_loop(0, GROUPS, rank_group, 0)

    def child_of(at_group, j):
        branch = j
        for k in range(ALIVE):
            branch = branch + jnp.where(alive_table[at_group * ALIVE + k] - k <= j, 1, 0)
        return jnp.minimum(branch, BR - 1)

    for half in range(2):
        for spread_at in range(SIDE):
            target = z * SIDE + spread_at if half == 0 else spread_at * SIDE + y

            def find_source(j, carry, half=half, spread_at=spread_at, target=target):
                parent = parent_ref[target * BR + child_of(target, j)]
                from_group = parent // BR
                rank = rank_table[parent]
                if half == 1:
                    from_group = (from_group % SIDE) * SIDE + from_group // SIDE
                source_table[(half * SIDE + spread_at) * KIDS + j] = from_group * ALIVE + rank
                return carry

            lax.fori_loop(0, KIDS, find_source, 0)

    def own_children(j, carry):
        child_table[j] = child_of(group, j)
        return carry

    lax.fori_loop(0, KIDS, own_children, 0)

    def own_slots(b, carry):
        rank = rank_table[group * BR + b]
        lives = surviving_ref[group * BR + b]
        slot_table[b] = jnp.minimum(jnp.where(lives > 0, rank, ALIVE + b - rank), SLOTS - 1)
        return carry

    lax.fori_loop(0, BR, own_slots, 0)
    pl.semaphore_wait(barrier, 2 * (SIDE - 1) + MP - 1)

    feature_copies = []
    for step in range(1, MP):
        copy = pltpu.make_async_remote_copy(
            src_ref=hidden_ref, dst_ref=features.at[part],
            send_sem=feature_send.at[step - 1], recv_sem=feature_recv.at[step - 1],
            device_id=(group, shifted(part, step, MP)), device_id_type=MESH)
        copy.start()
        feature_copies.append(copy)
    features[part] = hidden_ref[...]

    pool_copy.wait()
    weight_copies = []
    rows = hidden_ref.shape[1]
    for m in range(MP):
        some = pl.ds(m * rows, rows)
        copies = [
            pltpu.make_async_copy(source.at[some], target.at[some], weight_sem.at[m, i])
            for i, (source, target) in enumerate(
                ((w_query_ref, w_query), (w_key_ref, w_key), (w_value_ref, w_value)))
        ]
        for copy in copies:
            copy.start()
        weight_copies.append(copies)

    def remote(half, q, kind, source, target, gather_at, spread_at):
        return pltpu.make_async_remote_copy(
            src_ref=source, dst_ref=target,
            send_sem=send_sem.at[half, q, kind], recv_sem=recv_sem.at[half, q, kind],
            device_id=device(half, gather_at, spread_at), device_id_type=MESH)

    spread_copies, gather_copies, forward_copies, deliver_copies, out_copies = {}, {}, {}, {}, {}
    started = []

    for q in range(NQ):
        for half in range(2):
            def pack_alive(k, carry, q=q, half=half):
                branch = group * BR + jnp.minimum(alive_table[group * ALIVE + k], BR - 1)
                for spread_at in range(SIDE):
                    for r in range(PQ):
                        position = half * HALF + spread_at * PIECE + q * PQ + r
                        page = table_ref[position, branch]
                        arrived[half, q, spread_at, k, r] = pool[page]
                return carry

            lax.fori_loop(0, ALIVE, pack_alive, 0)
            a, c = along[half], across[half]
            here = pl.ds(a * 16 + c * 4, 4)
            copies = []
            for step in range(1, SIDE):
                to = shifted(c, step)
                copy = remote(
                    half, q, step - 1, arrived.at[half, q, to, pl.ds(0, ALIVE)], gathered[half][q].at[here], a, to)
                copy.start()
                copies.append(copy)
            gathered[half][q][here] = arrived[half, q, c, 0:ALIVE]
            spread_copies[half, q] = copies
            started += copies

    for q in range(NQ):
        for half in range(2):
            a, c = along[half], across[half]
            for copy in spread_copies[half, q]:
                copy.wait_recv()
            block = gathered[half][q].at[pl.ds(a * 16, 16)]
            copies = []
            for kind, step in ((3, 1), (4, -1)):
                copy = remote(half, q, kind, block, block, shifted(a, step), c)
                copy.start()
                copies.append(copy)
            gather_copies[half, q] = copies
            started += copies

    for copy in feature_copies:
        copy.wait_recv()
    project[...] = jnp.zeros_like(project)
    for m in range(MP):
        for copy in weight_copies[m]:
            copy.wait()
        some = pl.ds(m * rows, rows)
        part_rows = features[m]
        for i in range(4):
            columns = pl.ds(i * 256, 256)
            project[:, columns] += jnp.dot(
                part_rows, w_query[some, columns], preferred_element_type=jnp.float32)
        project[:, pl.ds(1024, HD)] += jnp.dot(part_rows, w_key[some], preferred_element_type=jnp.float32)
        project[:, pl.ds(1152, HD)] += jnp.dot(part_rows, w_value[some], preferred_element_type=jnp.float32)

    def normalize(block, gain):
        return block * lax.rsqrt(jnp.mean(block * block, -1, keepdims=True) + 1e-06) * gain

    for head in range(H // KVH):
        block = normalize(project[:, pl.ds(head * HD, HD)], query_gain_ref[...]) / math.sqrt(HD)
        queries[:, head, :] = block.astype(jnp.bfloat16).astype(jnp.float32)
    keys[:, 0, :] = normalize(project[:, pl.ds(1024, HD)], key_gain_ref[...]).astype(jnp.bfloat16).astype(jnp.float32)
    values[:, 0, :] = project[:, pl.ds(1152, HD)].astype(jnp.bfloat16).astype(jnp.float32)

    def slot_branch(slot):
        if slot < ALIVE:
            return jnp.minimum(alive_table[group * ALIVE + slot], BR - 1)
        return child_table[slot - ALIVE]

    branches = [slot_branch(slot) for slot in range(SLOTS)]
    for slot in range(SLOTS):
        branch = branches[slot]
        own_score = jnp.sum(queries[branch] * keys[branch], -1, keepdims=True)
        peak[slot] = jnp.broadcast_to(own_score, (H // KVH, HD))
        mass[slot] = jnp.ones((H // KVH, HD), jnp.float32)
        mixed[slot] = jnp.broadcast_to(values[branch], (H // KVH, HD))

    def attend(slot, window):
        tokens = window.reshape(CHUNK_TOKENS, 2 * HD)
        query = queries[branches[slot]].astype(jnp.bfloat16)
        scores = lax.dot_general(
            query, tokens[:, :HD], (((1,), (1,)), ((), ())), preferred_element_type=jnp.float32)
        old = peak[slot]
        new = jnp.maximum(old, jnp.max(scores, -1, keepdims=True))
        scale = jnp.exp(old - new)
        terms = jnp.exp(scores - new[:, :1])
        peak[slot] = new
        mass[slot] = mass[slot] * scale + jnp.sum(terms, -1, keepdims=True)
        mixed[slot] = mixed[slot] * scale + jnp.dot(
            terms.astype(jnp.bfloat16), tokens[:, HD:], preferred_element_type=jnp.float32)

    for q in range(NQ):
        for half in range(2):
            a, c = along[half], across[half]
            for copy in gather_copies[half, q]:
                copy.wait_recv()
            copies = []
            for kind, step, first in ((5, 1, 0), (6, -1, 8)):
                block = gathered[half][q].at[pl.ds(shifted(a, -step) * 16 + first, 8)]
                copy = remote(half, q, kind, block, block, shifted(a, step), c)
                copy.start()
                copies.append(copy)
            forward_copies[half, q] = copies
            started += copies

    for q in range(NQ):
        for half in range(2):
            for k in range(ALIVE):
                attend(k, arrived[half, q, :, k])

    for q in range(NQ):
        for half in range(2):
            a, c = along[half], across[half]
            for copy in forward_copies[half, q]:
                copy.wait_recv()
            for step in range(SIDE):
                to = shifted(c, step)

                def pack(j, carry, q=q, half=half, step=step, to=to):
                    source = source_table[(half * SIDE + to) * KIDS + j]
                    pages = gathered[half][q][source]
                    if step == 0:
                        arrived[half, q, to, ALIVE + j] = pages
                    else:
                        outgoing[half, q, step - 1, j] = pages
                    return carry

                lax.fori_loop(0, KIDS, pack, 0)
                if step:
                    copy = remote(
                        half, q, 6 + step, outgoing.at[half, q, step - 1],
                        arrived.at[half, q, c, pl.ds(ALIVE, KIDS)], a, to)
                    copy.start()
                    deliver_copies.setdefault((half, q), []).append(copy)
                    started.append(copy)

    for q in range(NQ):
        for half in range(2):
            for copy in deliver_copies[half, q]:
                copy.wait_recv()
            copy = pltpu.make_async_copy(arrived.at[half, q], arrived_out_ref.at[half, q], out_sem.at[half, q])
            copy.start()
            out_copies[half, q] = copy
            for j in range(KIDS):
                attend(ALIVE + j, arrived[half, q, :, ALIVE + j])

    for slot in range(SLOTS):
        mixed[slot] = mixed[slot] / mass[slot]
    for b in range(BR):
        result[b] = mixed[slot_table[b]]
    for head in range(H // KVH):
        attention_ref[:, pl.ds(head * HD, HD)] = result[:, head, :].astype(jnp.bfloat16)

    for copy in out_copies.values():
        copy.wait()
    for copy in started + feature_copies:
        copy.wait_send()


def refill_kernel(
    arrived_ref, table_ref, surviving_ref, refilled_ref, arrived, refilled, slot_table, in_sem, out_sem
):
    group = lax.axis_index("dp")
    loads = {}
    for q in range(NQ):
        for half in range(2):
            copy = pltpu.make_async_copy(arrived_ref.at[half, q], arrived.at[half, q], in_sem.at[half, q])
            copy.start()
            loads[half, q] = copy

    def find_slot(b, rank):
        lives = surviving_ref[group * BR + b] > 0
        slot_table[b] = jnp.minimum(jnp.where(lives, rank, ALIVE + b - rank), SLOTS - 1)
        return rank + jnp.where(lives, 1, 0)

    lax.fori_loop(0, BR, find_slot, jnp.int32(0))
    for (half, q), copy in loads.items():
        copy.wait()

        def place(b, carry, half=half, q=q):
            slot = slot_table[b]
            for c in range(SIDE):
                for r in range(PQ):
                    page = table_ref[half * HALF + c * PIECE + q * PQ + r, group * BR + b]
                    refilled[page] = arrived[half, q, c, slot, r]
            return carry

        lax.fori_loop(0, BR, place, 0)
    store = pltpu.make_async_copy(refilled, refilled_ref, out_sem)
    store.start()
    store.wait()


def shards(
    hidden, w_query, w_key, w_value, query_gain, key_gain, kv_pool, page_table, parent, surviving
):
    pool_pages = kv_pool.shape[0]
    pool = kv_pool.reshape(pool_pages, PAGE, 2 * HD)
    table = page_table.T
    vmem = pl.BlockSpec(memory_space=pltpu.VMEM)
    smem = pl.BlockSpec(memory_space=pltpu.SMEM)
    hbm = pl.BlockSpec(memory_space=pltpu.HBM)
    bf16, f32 = jnp.bfloat16, jnp.float32
    page_shape = (PAGE, 2 * HD)
    heads = H // KVH
    arrived, attention = pl.pallas_call(
        relay_kernel,
        out_shape=(
            jax.ShapeDtypeStruct((2, NQ, SIDE, SLOTS, PQ) + page_shape, bf16),
            jax.ShapeDtypeStruct((BR, heads * HD), bf16),
        ),
        in_specs=[vmem] * 3 + [hbm] * 4 + [smem] * 3,
        out_specs=(hbm, vmem),
        scratch_shapes=[pltpu.VMEM((GROUPS * ALIVE, PQ) + page_shape, bf16)] * (2 * NQ)
        + [
            pltpu.VMEM((2, NQ, SIDE - 1, KIDS, PQ) + page_shape, bf16),
            pltpu.VMEM((2, NQ, SIDE, SLOTS, PQ) + page_shape, bf16),
            pltpu.VMEM(pool.shape, bf16),
            pltpu.VMEM((MP,) + hidden.shape, bf16),
            pltpu.VMEM(w_query.shape, bf16),
            pltpu.VMEM(w_key.shape, bf16),
            pltpu.VMEM(w_value.shape, bf16),
            pltpu.VMEM((BR, heads * HD + 2 * HD), f32),
            pltpu.VMEM((BR, heads, HD), f32),
            pltpu.VMEM((BR, 1, HD), f32),
            pltpu.VMEM((BR, 1, HD), f32),
            pltpu.VMEM((SLOTS, heads, HD), f32),
            pltpu.VMEM((SLOTS, heads, HD), f32),
            pltpu.VMEM((SLOTS, heads, HD), f32),
            pltpu.VMEM((BR, heads, HD), f32),
            pltpu.SMEM((GROUPS * ALIVE,), jnp.int32),
            pltpu.SMEM((GROUPS * BR,), jnp.int32),
            pltpu.SMEM((2 * SIDE * KIDS,), jnp.int32),
            pltpu.SMEM((KIDS,), jnp.int32),
            pltpu.SMEM((BR,), jnp.int32),
            pltpu.SemaphoreType.DMA((2, NQ, 10)),
            pltpu.SemaphoreType.DMA((2, NQ, 10)),
            pltpu.SemaphoreType.DMA((MP - 1,)),
            pltpu.SemaphoreType.DMA((MP - 1,)),
            pltpu.SemaphoreType.DMA,
            pltpu.SemaphoreType.DMA((MP, 3)),
            pltpu.SemaphoreType.DMA((2, NQ)),
        ],
        compiler_params=pltpu.CompilerParams(
            collective_id=0, has_side_effects=True, vmem_limit_bytes=56 * 2**20),
        name="relay_pages_and_attend",
    )(
        hidden, query_gain.reshape(1, HD), key_gain.reshape(1, HD), w_query, w_key, w_value, pool,
        table, parent, surviving,
    )
    refilled = pl.pallas_call(
        refill_kernel,
        out_shape=jax.ShapeDtypeStruct(pool.shape, bf16),
        in_specs=[hbm, smem, smem],
        out_specs=hbm,
        scratch_shapes=[
            pltpu.VMEM(arrived.shape, bf16),
            pltpu.VMEM(pool.shape, bf16),
            pltpu.SMEM((BR,), jnp.int32),
            pltpu.SemaphoreType.DMA((2, NQ)),
            pltpu.SemaphoreType.DMA,
        ],
        compiler_params=pltpu.CompilerParams(vmem_limit_bytes=56 * 2**20),
        name="refill_pool",
    )(arrived, table, surviving)
    return (refilled.reshape(kv_pool.shape), attention)


def solution(mesh):
    return jax.shard_map(
        shards,
        mesh=mesh,
        in_specs=(
            P("dp", "mp"),
            P(None, "mp"),
            P(None, "mp"),
            P(None, "mp"),
            P(),
            P(),
            P("dp", None, "mp", None),
            P(),
            P(),
            P(),
        ),
        out_specs=(P("dp", None, "mp", None), P("dp", "mp")),
        check_vma=False,
    )
```

time: 266 us -> 98.2 us (0.37)
  waiting for transfers between devices: 157 us -> 0 us
  Pallas kernels: 0 us -> 95.1 us
  matrix products: 31.8 us -> 0 us
  other arithmetic: 29.8 us -> 0 us
  local copies, waits for them, and re-layouts: 22.7 us -> 0.62 us
  blocking collectives: 13.9 us -> 0 us
  starting transfers between devices: 8.77 us -> 0 us
    all_to_all x1 -> x0, waiting for transfers between devices: 157 us -> none  [shards(): lax.all_to_all(packed, 'dp', split_axis=0, concat_axis=0, tiled=True)]
    pallas_call x0 -> x2, Pallas kernels: none -> 95.1 us  [the longest x1 87.4 us: shards(): pl.pallas_call(relay_kernel, out_shape=(jax.ShapeDtypeStruct((2, NQ, SIDE...]
    dot_general x8 -> x0, matrix products: 31.8 us -> none  [the longest x2 14.8 us: attend_sets(): jnp.einsum('nkgd,tkd->nkgt', query_rows, tokens[..., :HD], preferred_elem...]
    gather x3 -> x0, local copies, waits for them, and re-layouts: 19.9 us -> none  [the longest x2 10.2 us: shards(): packed = kv_pool[page_table[parent_slot]]]
    all_gather x1 -> x0, blocking collectives: 13.9 us -> none  [shards(): features = lax.all_gather(hidden, 'mp', axis=1, tiled=True)]
    reduce_sum x7 -> x0, other arithmetic: 12.1 us -> none  [the longest x2 10.4 us: attend_sets(): total_mass = total_mass + jnp.sum(expo_terms, -1)]
    select_n x7 -> x0, other arithmetic: 9.29 us -> none  [the longest x1 9.21 us: shards(): refilled = jnp.where(owner_child[:, None, None, None], moved_pages, kv_pool)]
    all_to_all x1 -> x0, starting transfers between devices: 8.77 us -> none  [shards(): lax.all_to_all(packed, 'dp', split_axis=0, concat_axis=0, tiled=True)]
  transfers between devices with their start and end apart: 1 -> 0, of which waited for: 1 -> 0; matrix products, arithmetic and copies ran while one was open for 6% -> 0% of each run, Pallas kernels for 0% -> 0%
where the time goes in v1:
time: 98.2 us; the launch traced here: 96.4 us
  Pallas kernels  95.1 us (97%)
    pallas_call x1, Pallas kernels, shards(): pl.pallas_call(relay_kernel, out_shape=(jax.ShapeDtypeStruct((2, NQ, SIDE...  87.4 us
    pallas_call x1, Pallas kernels, shards(): pl.pallas_call(refill_kernel, out_shape=jax.ShapeDtypeStruct(pool.shape,...  7.7 us

profile of v1, /device:TPU:1, one launch (start us, length us, event | category | flops | bytes accessed | tf_op | source)
XLA Modules:
  0.0 96.4 jit_solution(15663450684625696063)
XLA Ops:
  0.6 87.4 %relay_pages_and_attend.1 = (bf16[2,3,4,18,2,16,256]{6,5,4,3,2,1,0:T(8,128)(2,1)}, bf16[16,1024]{1,0:T(8,128)(2,1)}) custom-call(bf16[16,640]{1,0:T(8,128)(2,1)} %hidden_ref.1, f32[1,128]{1,0:T(1,128)} %bitcast.11, f32[1,128]{1,0:T(1,128)} %bitcast.12, bf16[5120,1024]{1,0:T(8,128)(2,1)} %w_query_ref.1, bf16[5120,128]{1,0:T(8,128)(2,1)} %w_key_ref.1, ...), custom_call_target="tpu_custom_call" | custom-call | tf_op jit(solution)/shard_map/relay_pages_and_attend/pallas_call | solution.py:355
  88.1 0.0 copy-start
  88.1 7.7 %refill_pool.1 = bf16[768,16,256]{2,1,0:T(8,128)(2,1)} custom-call(bf16[2,3,4,18,2,16,256]{6,5,4,3,2,1,0:T(8,128)(2,1)} %get-tuple-element.4.arrived_ref, s32[48,256]{1,0:T(8,128)} %bitcast.10, s32[256]{0:T(256)} %surviving_ref.3), custom_call_target="tpu_custom_call" | custom-call | tf_op jit(solution)/shard_map/refill_pool/pallas_call | solution.py:400
  95.8 0.0 copy-done
  95.8 0.6 copy.14
Async XLA Ops:
  88.1 7.7 %copy-start = (bf16[16,1024]{1,0:T(8,128)(2,1)S(1)}, bf16[16,1024]{1,0:T(8,128)(2,1)}, u32[]{:S(2)}) copy-start(bf16[16,1024]{1,0:T(8,128)(2,1)} %get-tuple-element.11) | copy-start | bytes 98308

commit v2 on v1

v2 whole, which is shorter than its diff:
```python
import math

import jax
import jax.numpy as jnp
from jax import lax
from jax.experimental import pallas as pl
from jax.experimental.pallas import tpu as pltpu
from jax.sharding import PartitionSpec as P

H = 64
KVH = 8
HD = 128
PAGE = 16
NPAGE = 48
BR = 16
GROUPS = 16
ALIVE = 4
KIDS = 14
SIDE = 4
NQ = 3
PQ = 2
PIECE = NQ * PQ
HALF = NPAGE // 2
MP = 8
MESH = pl.DeviceIdType.MESH
SLOTS = ALIVE + KIDS
CHUNK_TOKENS = SIDE * PQ * PAGE
HEADS = H // KVH
RANGES = 6


def attend_chunk(arrived, queries, scores, terms, mixes, peak, mass, mixed, q, first, count):
    rows = pl.ds(first * HEADS, count * HEADS)
    windows = [
        [arrived[half, q, :, first + j].reshape(CHUNK_TOKENS, 2 * HD) for half in range(2)] for j in range(count)
    ]
    for j in range(count):
        query = queries[pl.ds((first + j) * HEADS, HEADS)].astype(jnp.bfloat16)
        for half in range(2):
            scores[pl.ds(j * HEADS, HEADS), pl.ds(half * CHUNK_TOKENS, CHUNK_TOKENS)] = lax.dot_general(
                query, windows[j][half][:, :HD], (((1,), (1,)), ((), ())), preferred_element_type=jnp.float32)
    part = pl.ds(0, count * HEADS)
    all_scores = scores[part]
    old = peak[rows]
    new = jnp.maximum(old, jnp.max(all_scores, -1, keepdims=True))
    scale = jnp.exp(old - new)
    all_terms = jnp.exp(all_scores - new[:, :1])
    terms[part] = all_terms
    for j in range(count):
        total = jnp.zeros((HEADS, HD), jnp.float32)
        for half in range(2):
            weights = terms[pl.ds(j * HEADS, HEADS), pl.ds(half * CHUNK_TOKENS, CHUNK_TOKENS)].astype(jnp.bfloat16)
            total += jnp.dot(weights, windows[j][half][:, HD:], preferred_element_type=jnp.float32)
        mixes[pl.ds(j * HEADS, HEADS)] = total
    new_mass = mass[rows] * scale + jnp.sum(all_terms, -1, keepdims=True)
    return new, new_mass, mixed[rows] * scale + mixes[part]


def relay_kernel(
    hidden_ref, query_gain_hbm, key_gain_hbm, w_query_ref, w_key_ref, w_value_ref, pool_ref,
    table_hbm, parent_hbm, surviving_hbm,
    arrived, slot_queries, peak, mass, mixed, places_ref,
    *scratch,
):
    scratch = list(scratch)
    gathered = [[scratch.pop(0) for _ in range(NQ)] for _ in range(2)]
    (outgoing, pool, features, w_query, w_key, w_value, project, queries, keys, values,
     scores, terms, mixes,
     query_gain_ref, key_gain_ref, table_ref, parent_ref, surviving_ref,
     alive_table, rank_table, source_table, child_table, slot_table,
     send_sem, recv_sem, feature_send, feature_recv, pool_sem, weight_sem, small_sem) = scratch

    group = lax.axis_index("dp")
    part = lax.axis_index("mp")
    z, y = group // SIDE, group % SIDE
    along = [z, y]
    across = [y, z]

    def device(half, gather_at, spread_at):
        if half == 0:
            return (gather_at * SIDE + spread_at, part)
        return (spread_at * SIDE + gather_at, part)

    def shifted(value, step, size=SIDE):
        return (value + step + size) % size

    pool_copy = pltpu.make_async_copy(pool_ref, pool, pool_sem)
    small_copies = [
        pltpu.make_async_copy(source, target, small_sem.at[i])
        for i, (source, target) in enumerate((
            (surviving_hbm, surviving_ref), (parent_hbm, parent_ref), (table_hbm, table_ref),
            (query_gain_hbm, query_gain_ref), (key_gain_hbm, key_gain_ref),
            (hidden_ref, features.at[part])))
    ]
    for copy in small_copies:
        copy.start()
    pool_copy.start()

    barrier = pltpu.get_barrier_semaphore()
    for step in range(1, SIDE):
        pl.semaphore_signal(barrier, inc=1, device_id=device(0, z, shifted(y, step)), device_id_type=MESH)
        pl.semaphore_signal(barrier, inc=1, device_id=device(1, y, shifted(z, step)), device_id_type=MESH)
    for step in range(1, MP):
        pl.semaphore_signal(barrier, inc=1, device_id=(group, shifted(part, step, MP)), device_id_type=MESH)

    def rank_group(at, carry):
        found = [jnp.int32(99) for _ in range(ALIVE)]
        count = jnp.int32(0)
        for branch in range(BR):
            lives = surviving_ref[at * BR + branch]
            rank_table[at * BR + branch] = count
            for k in range(ALIVE):
                found[k] = jnp.where((lives > 0) & (count == k), jnp.int32(branch), found[k])
            count = count + lives
        for k in range(ALIVE):
            alive_table[at * ALIVE + k] = found[k]
        return carry

    def child_of(at_group, j):
        branch = j
        for k in range(ALIVE):
            branch = branch + jnp.where(alive_table[at_group * ALIVE + k] - k <= j, 1, 0)
        return jnp.minimum(branch, BR - 1)

    def find_sources():
        for half in range(2):
            for spread_at in range(SIDE):
                target = z * SIDE + spread_at if half == 0 else spread_at * SIDE + y

                def find_source(j, carry, half=half, spread_at=spread_at, target=target):
                    parent = parent_ref[target * BR + child_of(target, j)]
                    from_group = parent // BR
                    rank = rank_table[parent]
                    if half == 1:
                        from_group = (from_group % SIDE) * SIDE + from_group // SIDE
                    source_table[(half * SIDE + spread_at) * KIDS + j] = from_group * ALIVE + rank
                    return carry

                lax.fori_loop(0, KIDS, find_source, 0)

        def own_children(j, carry):
            child_table[j] = child_of(group, j)
            return carry

        lax.fori_loop(0, KIDS, own_children, 0)

        def own_slots(b, carry):
            rank = rank_table[group * BR + b]
            lives = surviving_ref[group * BR + b]
            slot_table[b] = jnp.minimum(jnp.where(lives > 0, rank, ALIVE + b - rank), SLOTS - 1)
            return carry

        lax.fori_loop(0, BR, own_slots, 0)

    def invert_table():
        row = lax.broadcasted_iota(jnp.int32, (8, 128), 0)
        lane = lax.broadcasted_iota(jnp.int32, (8, 128), 1)
        page_ids = row * 128 + lane

        def one_branch(b, places):
            slot = slot_table[b]
            places = jnp.where((row == 7) & (lane == b), slot, places)
            for half in range(2):
                for c in range(SIDE):
                    for q in range(NQ):
                        for r in range(PQ):
                            page = table_ref[half * HALF + c * PIECE + q * PQ + r, group * BR + b]
                            place = (((half * NQ + q) * SIDE + c) * SLOTS + slot) * PQ + r
                            places = jnp.where(page_ids == page, place, places)
            return places

        places_ref[...] = lax.fori_loop(0, BR, one_branch, jnp.zeros((8, 128), jnp.int32))

    feature_copies, weight_copies = [], []
    rows = hidden_ref.shape[1]

    def send_features():
        for step in range(1, MP):
            copy = pltpu.make_async_remote_copy(
                src_ref=hidden_ref, dst_ref=features.at[part],
                send_sem=feature_send.at[step - 1], recv_sem=feature_recv.at[step - 1],
                device_id=(group, shifted(part, step, MP)), device_id_type=MESH)
            copy.start()
            feature_copies.append(copy)

    def load_weights():
        for m in range(MP):
            some = pl.ds(m * rows, rows)
            copies = [
                pltpu.make_async_copy(source.at[some], target.at[some], weight_sem.at[m, i])
                for i, (source, target) in enumerate(
                    ((w_query_ref, w_query), (w_key_ref, w_key), (w_value_ref, w_value)))
            ]
            for copy in copies:
                copy.start()
            weight_copies.append(copies)

    def remote(half, q, kind, source, target, gather_at, spread_at):
        return pltpu.make_async_remote_copy(
            src_ref=source, dst_ref=target,
            send_sem=send_sem.at[half, q, kind], recv_sem=recv_sem.at[half, q, kind],
            device_id=device(half, gather_at, spread_at), device_id_type=MESH)

    spread_copies, gather_copies, forward_copies, deliver_copies = {}, {}, {}, {}
    started = []

    def pack_alive(q):
        def one(k, carry):
            branch = group * BR + jnp.minimum(alive_table[group * ALIVE + k], BR - 1)
            for half in range(2):
                for spread_at in range(SIDE):
                    for r in range(PQ):
                        page = table_ref[half * HALF + spread_at * PIECE + q * PQ + r, branch]
                        arrived[half, q, spread_at, k, r] = pool[page]
            return carry

        lax.fori_loop(0, ALIVE, one, 0)

    def spread(q):
        for half in range(2):
            a, c = along[half], across[half]
            here = pl.ds(a * 16 + c * 4, 4)
            copies = []
            for step in (1, 3, 2):
                to = shifted(c, step)
                copy = remote(
                    half, q, step - 1, arrived.at[half, q, to, pl.ds(0, ALIVE)], gathered[half][q].at[here], a, to)
                copy.start()
                copies.append(copy)
            gathered[half][q][here] = arrived[half, q, c, 0:ALIVE]
            spread_copies[half, q] = copies
            started.extend(copies)

    def gather(q):
        for half in range(2):
            a, c = along[half], across[half]
            for copy in spread_copies[half, q]:
                copy.wait_recv()
            block = gathered[half][q].at[pl.ds(a * 16, 16)]
            copies = []
            for kind, step in ((3, 1), (4, -1)):
                copy = remote(half, q, kind, block, block, shifted(a, step), c)
                copy.start()
                copies.append(copy)
            gather_copies[half, q] = copies
            started.extend(copies)

    def forward(q):
        for half in range(2):
            a, c = along[half], across[half]
            for copy in gather_copies[half, q]:
                copy.wait_recv()
            copies = []
            for kind, step, first in ((5, 1, 0), (6, -1, 8)):
                block = gathered[half][q].at[pl.ds(shifted(a, -step) * 16 + first, 8)]
                copy = remote(half, q, kind, block, block, shifted(a, step), c)
                copy.start()
                copies.append(copy)
            forward_copies[half, q] = copies
            started.extend(copies)

    def deliver(q):
        for half in range(2):
            a, c = along[half], across[half]
            for copy in forward_copies[half, q]:
                copy.wait_recv()
            deliver_copies[half, q] = []
            for step in (1, 3, 2, 0):
                to = shifted(c, step)

                def pack(j, carry, half=half, step=step, to=to):
                    pages = gathered[half][q][source_table[(half * SIDE + to) * KIDS + j]]
                    if step == 0:
                        arrived[half, q, to, ALIVE + j] = pages
                    else:
                        outgoing[half, q, step - 1, j] = pages
                    return carry

                lax.fori_loop(0, KIDS, pack, 0)
                if step:
                    copy = remote(
                        half, q, 6 + step, outgoing.at[half, q, step - 1],
                        arrived.at[half, q, c, pl.ds(ALIVE, KIDS)], a, to)
                    copy.start()
                    deliver_copies[half, q].append(copy)
                    started.append(copy)

    def normalize(block, gain):
        return block * lax.rsqrt(jnp.mean(block * block, -1, keepdims=True) + 1e-06) * gain

    def project_tokens():
        for copy in small_copies[3:]:
            copy.wait()
        for copy in feature_copies:
            copy.wait_recv()
        project[...] = jnp.zeros_like(project)
        for m in range(MP):
            for copy in weight_copies[m]:
                copy.wait()
            some = pl.ds(m * rows, rows)
            part_rows = features[m]
            for i in range(4):
                columns = pl.ds(i * 256, 256)
                project[:, columns] += jnp.dot(
                    part_rows, w_query[some, columns], preferred_element_type=jnp.float32)
            project[:, pl.ds(1024, HD)] += jnp.dot(part_rows, w_key[some], preferred_element_type=jnp.float32)
            project[:, pl.ds(1152, HD)] += jnp.dot(part_rows, w_value[some], preferred_element_type=jnp.float32)
        for head in range(HEADS):
            block = normalize(project[:, pl.ds(head * HD, HD)], query_gain_ref[...]) / math.sqrt(HD)
            queries[:, head, :] = block.astype(jnp.bfloat16).astype(jnp.float32)
        key_rows = normalize(project[:, pl.ds(1024, HD)], key_gain_ref[...])
        keys[:, 0, :] = key_rows.astype(jnp.bfloat16).astype(jnp.float32)
        values[:, 0, :] = project[:, pl.ds(1152, HD)].astype(jnp.bfloat16).astype(jnp.float32)

    def start_attention():
        for slot in range(SLOTS):
            if slot < ALIVE:
                branch = jnp.minimum(alive_table[group * ALIVE + slot], BR - 1)
            else:
                branch = child_table[slot - ALIVE]
            some = pl.ds(slot * HEADS, HEADS)
            query = queries[branch]
            slot_queries[some] = query
            own_score = jnp.sum(query * keys[branch], -1, keepdims=True)
            peak[some] = jnp.broadcast_to(own_score, (HEADS, HD))
            mass[some] = jnp.ones((HEADS, HD), jnp.float32)
            mixed[some] = jnp.broadcast_to(values[branch], (HEADS, HD))

    def attend(q, first, count):
        some = pl.ds(first * HEADS, count * HEADS)
        peak[some], mass[some], mixed[some] = attend_chunk(
            arrived, slot_queries, scores, terms, mixes, peak, mass, mixed, q, first, count)

    small_copies[0].wait()
    lax.fori_loop(0, GROUPS, rank_group, 0)
    small_copies[1].wait()
    find_sources()
    small_copies[2].wait()
    pool_copy.wait()
    pack_alive(0)
    pl.semaphore_wait(barrier, 2 * (SIDE - 1) + MP - 1)
    spread(0)
    for q in range(1, NQ):
        pack_alive(q)
        spread(q)
    send_features()
    load_weights()
    for q in range(NQ):
        gather(q)
    invert_table()
    for q in range(NQ):
        forward(q)
    for q in range(NQ):
        deliver(q)
    project_tokens()
    start_attention()
    for q in range(NQ):
        attend(q, 0, ALIVE)
    for q in range(NQ):
        for half in range(2):
            for copy in deliver_copies[half, q]:
                copy.wait_recv()
        if q < NQ - 1:
            attend(q, ALIVE, KIDS)
    for copy in started + feature_copies:
        copy.wait_send()


def refill_kernel(
    arrived, slot_queries, peak, mass, mixed, places_ref,
    refilled_ref, attention_ref,
    refilled, scores, terms, mixes, final, result, store_sem,
):
    pages = arrived.reshape(2 * NQ * SIDE * SLOTS * PQ, PAGE, 2 * HD)
    stores = []
    for part in range(RANGES):
        def place(i, carry, part=part):
            refilled[part * 128 + i] = pages[places_ref[part, i]]
            return carry

        lax.fori_loop(0, 128, place, 0, unroll=8)
        some = pl.ds(part * 128, 128)
        copy = pltpu.make_async_copy(refilled.at[some], refilled_ref.at[some], store_sem.at[part])
        copy.start()
        stores.append(copy)
    alive = pl.ds(0, ALIVE * HEADS)
    final[alive] = mixed[alive] / mass[alive]
    _, total, mix = attend_chunk(
        arrived, slot_queries, scores, terms, mixes, peak, mass, mixed, NQ - 1, ALIVE, KIDS)
    final[pl.ds(ALIVE * HEADS, KIDS * HEADS)] = mix / total
    for b in range(BR):
        result[b] = final[pl.ds(pl.multiple_of(places_ref[7, b] * HEADS, HEADS), HEADS)]
    for head in range(HEADS):
        attention_ref[:, pl.ds(head * HD, HD)] = result[:, head, :].astype(jnp.bfloat16)
    for copy in stores:
        copy.wait()


def shards(
    hidden, w_query, w_key, w_value, query_gain, key_gain, kv_pool, page_table, parent, surviving
):
    pool_pages = kv_pool.shape[0]
    pool = kv_pool.reshape(pool_pages, PAGE, 2 * HD)
    table = page_table.T
    vmem = pl.BlockSpec(memory_space=pltpu.VMEM)
    smem = pl.BlockSpec(memory_space=pltpu.SMEM)
    hbm = pl.BlockSpec(memory_space=pltpu.HBM)
    bf16, f32, i32 = jnp.bfloat16, jnp.float32, jnp.int32
    page_shape = (PAGE, 2 * HD)
    state = pltpu.VMEM((SLOTS * HEADS, HD), f32)
    chunk = [
        pltpu.VMEM((KIDS * HEADS, 2 * CHUNK_TOKENS), f32),
        pltpu.VMEM((KIDS * HEADS, 2 * CHUNK_TOKENS), f32),
        pltpu.VMEM((KIDS * HEADS, HD), f32),
    ]
    operands = [
        pltpu.with_memory_space_constraint(x, pltpu.HBM)
        for x in (hidden, query_gain.reshape(1, HD), key_gain.reshape(1, HD), w_query, w_key, w_value, pool,
                  table, parent, surviving)
    ]
    *kept, places = pl.pallas_call(
        relay_kernel,
        out_shape=(
            pltpu.VMEM((2, NQ, SIDE, SLOTS, PQ) + page_shape, bf16),
            state, state, state, state,
            jax.ShapeDtypeStruct((8, 128), i32),
        ),
        in_specs=[hbm] * 10,
        out_specs=(vmem,) * 6,
        scratch_shapes=[pltpu.VMEM((GROUPS * ALIVE, PQ) + page_shape, bf16)] * (2 * NQ)
        + [
            pltpu.VMEM((2, NQ, SIDE - 1, KIDS, PQ) + page_shape, bf16),
            pltpu.VMEM(pool.shape, bf16),
            pltpu.VMEM((MP,) + hidden.shape, bf16),
            pltpu.VMEM(w_query.shape, bf16),
            pltpu.VMEM(w_key.shape, bf16),
            pltpu.VMEM(w_value.shape, bf16),
            pltpu.VMEM((BR, HEADS * HD + 2 * HD), f32),
            pltpu.VMEM((BR, HEADS, HD), f32),
            pltpu.VMEM((BR, 1, HD), f32),
            pltpu.VMEM((BR, 1, HD), f32),
            *chunk,
            pltpu.VMEM((1, HD), f32),
            pltpu.VMEM((1, HD), f32),
            pltpu.SMEM(table.shape, i32),
            pltpu.SMEM(parent.shape, i32),
            pltpu.SMEM(surviving.shape, i32),
            pltpu.SMEM((GROUPS * ALIVE,), i32),
            pltpu.SMEM((GROUPS * BR,), i32),
            pltpu.SMEM((2 * SIDE * KIDS,), i32),
            pltpu.SMEM((KIDS,), i32),
            pltpu.SMEM((BR,), i32),
            pltpu.SemaphoreType.DMA((2, NQ, 10)),
            pltpu.SemaphoreType.DMA((2, NQ, 10)),
            pltpu.SemaphoreType.DMA((MP - 1,)),
            pltpu.SemaphoreType.DMA((MP - 1,)),
            pltpu.SemaphoreType.DMA,
            pltpu.SemaphoreType.DMA((MP, 3)),
            pltpu.SemaphoreType.DMA((6,)),
        ],
        compiler_params=pltpu.CompilerParams(
            collective_id=0, has_side_effects=True, vmem_limit_bytes=44 * 2**20),
        name="relay_pages_and_attend",
    )(*operands)
    refilled, attention = pl.pallas_call(
        refill_kernel,
        out_shape=(
            jax.ShapeDtypeStruct(pool.shape, bf16),
            jax.ShapeDtypeStruct((BR, HEADS * HD), bf16),
        ),
        in_specs=[vmem] * 5 + [smem],
        out_specs=(hbm, vmem),
        scratch_shapes=[
            pltpu.VMEM(pool.shape, bf16),
            *chunk,
            pltpu.VMEM((SLOTS * HEADS, HD), f32),
            pltpu.VMEM((BR, HEADS, HD), f32),
            pltpu.SemaphoreType.DMA((RANGES,)),
        ],
        compiler_params=pltpu.CompilerParams(vmem_limit_bytes=44 * 2**20),
        name="refill_pool",
    )(*kept, places)
    return (refilled.reshape(kv_pool.shape), attention)


def solution(mesh):
    return jax.shard_map(
        shards,
        mesh=mesh,
        in_specs=(
            P("dp", "mp"),
            P(None, "mp"),
            P(None, "mp"),
            P(None, "mp"),
            P(),
            P(),
            P("dp", None, "mp", None),
            P(),
            P(),
            P(),
        ),
        out_specs=(P("dp", None, "mp", None), P("dp", "mp")),
        check_vma=False,
    )
```

time: 98.2 us -> 81.3 us (0.83); the launches traced: 96.4 us -> 81.2 us
  Pallas kernels: 95.1 us -> 80.5 us
    pallas_call x2, Pallas kernels: 95.1 us -> 80.5 us  [the longest x1 75.3 us: shards(): pl.pallas_call(relay_kernel, out_shape=(pltpu.VMEM((2, NQ, SIDE, SLOTS, P...]
where the time goes in v2:
time: 81.3 us; the launch traced here: 81.2 us
  Pallas kernels  80.5 us (99%)
    pallas_call x1, Pallas kernels, shards(): pl.pallas_call(relay_kernel, out_shape=(pltpu.VMEM((2, NQ, SIDE, SLOTS, P...  75.3 us
    pallas_call x1, Pallas kernels, shards(): pl.pallas_call(refill_kernel, out_shape=(jax.ShapeDtypeStruct(pool.shape,...  5.25 us

profile of v2, /device:TPU:1, one launch (start us, length us, event | category | flops | bytes accessed | tf_op | source)
XLA Modules:
  0.0 81.2 jit_solution(14253875552386558222)
XLA Ops:
  0.6 75.3 %relay_pages_and_attend.1 = (bf16[2,3,4,18,2,16,256]{6,5,4,3,2,1,0:T(8,128)(2,1)S(1)}, f32[144,128]{1,0:T(8,128)S(1)}, f32[144,128]{1,0:T(8,128)S(1)}, f32[144,1...) custom-call(bf16[16,640]{1,0:T(8,128)(2,1)} %hidden_ref.1, f32[1,128]{1,0:T(1,128)} %bitcast.9, ...), custom_call_target="tpu_custom_call" | custom-call | tf_op jit(solution)/shard_map/relay_pages_and_attend/pallas_call | solution.py:421
  75.9 5.3 %refill_pool.1 = (bf16[768,16,256]{2,1,0:T(8,128)(2,1)}, bf16[16,1024]{1,0:T(8,128)(2,1)}) custom-call(bf16[2,3,4,18,2,16,256]{6,5,4,3,2,1,0:T(8,128)(2,1)S(1)} %get-tuple-element.10.arrived, f32[144,128]{1,0:T(8,128)S(1)} %get-tuple-element.11.slot_queries, f32[144,128]{1,0:T(8,128)S(1)} %get-tuple-element.12.peak, f32[144,128]{1,0:T(8,128)S(1)} %get-tuple-element.13.mass, ...), custom_call_target="tpu_custom_call" | custom-call | tf_op jit(solution)/shard_map/refill_pool/pallas_call | solution.py:465

commit v3 on v2

--- a/solution.py
+++ b/solution.py
@@ -26,19 +26,21 @@
 SLOTS = ALIVE + KIDS
 CHUNK_TOKENS = SIDE * PQ * PAGE
 HEADS = H // KVH
-RANGES = 6
+RANGES = 12
+BATCH = 7
 
 
 def attend_chunk(arrived, queries, scores, terms, mixes, peak, mass, mixed, q, first, count):
     rows = pl.ds(first * HEADS, count * HEADS)
     windows = [
-        [arrived[half, q, :, first + j].reshape(CHUNK_TOKENS, 2 * HD) for half in range(2)] for j in range(count)
+        jnp.concatenate(
+            [arrived[half, q, :, first + j].reshape(CHUNK_TOKENS, 2 * HD) for half in range(2)], axis=0)
+        for j in range(count)
     ]
     for j in range(count):
         query = queries[pl.ds((first + j) * HEADS, HEADS)].astype(jnp.bfloat16)
-        for half in range(2):
-            scores[pl.ds(j * HEADS, HEADS), pl.ds(half * CHUNK_TOKENS, CHUNK_TOKENS)] = lax.dot_general(
-                query, windows[j][half][:, :HD], (((1,), (1,)), ((), ())), preferred_element_type=jnp.float32)
+        scores[pl.ds(j * HEADS, HEADS)] = lax.dot_general(
+            query, windows[j][:, :HD], (((1,), (1,)), ((), ())), preferred_element_type=jnp.float32)
     part = pl.ds(0, count * HEADS)
     all_scores = scores[part]
     old = peak[rows]
@@ -47,11 +49,9 @@
     all_terms = jnp.exp(all_scores - new[:, :1])
     terms[part] = all_terms
     for j in range(count):
-        total = jnp.zeros((HEADS, HD), jnp.float32)
-        for half in range(2):
-            weights = terms[pl.ds(j * HEADS, HEADS), pl.ds(half * CHUNK_TOKENS, CHUNK_TOKENS)].astype(jnp.bfloat16)
-            total += jnp.dot(weights, windows[j][half][:, HD:], preferred_element_type=jnp.float32)
-        mixes[pl.ds(j * HEADS, HEADS)] = total
+        weights = terms[pl.ds(j * HEADS, HEADS)].astype(jnp.bfloat16)
+        mixes[pl.ds(j * HEADS, HEADS)] = jnp.dot(
+            weights, windows[j][:, HD:], preferred_element_type=jnp.float32)
     new_mass = mass[rows] * scale + jnp.sum(all_terms, -1, keepdims=True)
     return new, new_mass, mixed[rows] * scale + mixes[part]
 
@@ -84,7 +84,10 @@
     def shifted(value, step, size=SIDE):
         return (value + step + size) % size
 
-    pool_copy = pltpu.make_async_copy(pool_ref, pool, pool_sem)
+    pool_copies = [
+        pltpu.make_async_copy(pool_ref.at[pl.ds(i * 64, 64)], pool.at[pl.ds(i * 64, 64)], pool_sem.at[i])
+        for i in range(RANGES)
+    ]
     small_copies = [
         pltpu.make_async_copy(source, target, small_sem.at[i])
         for i, (source, target) in enumerate((
@@ -94,7 +97,8 @@
     ]
     for copy in small_copies:
         copy.start()
-    pool_copy.start()
+    for copy in pool_copies:
+        copy.start()
 
     barrier = pltpu.get_barrier_semaphore()
     for step in range(1, SIDE):
@@ -208,10 +212,11 @@
         def one(k, carry):
             branch = group * BR + jnp.minimum(alive_table[group * ALIVE + k], BR - 1)
             for half in range(2):
-                for spread_at in range(SIDE):
-                    for r in range(PQ):
-                        page = table_ref[half * HALF + spread_at * PIECE + q * PQ + r, branch]
-                        arrived[half, q, spread_at, k, r] = pool[page]
+                where = [(spread_at, r) for spread_at in range(SIDE) for r in range(PQ)]
+                pages = [table_ref[half * HALF + spread_at * PIECE + q * PQ + r, branch] for spread_at, r in where]
+                blocks = [pool[page] for page in pages]
+                for (spread_at, r), block in zip(where, blocks):
+                    arrived[half, q, spread_at, k, r] = block
             return carry
 
         lax.fori_loop(0, ALIVE, one, 0)
@@ -221,7 +226,7 @@
             a, c = along[half], across[half]
             here = pl.ds(a * 16 + c * 4, 4)
             copies = []
-            for step in (1, 3, 2):
+            for step in (2, 1, 3):
                 to = shifted(c, step)
                 copy = remote(
                     half, q, step - 1, arrived.at[half, q, to, pl.ds(0, ALIVE)], gathered[half][q].at[here], a, to)
@@ -265,18 +270,21 @@
             for copy in forward_copies[half, q]:
                 copy.wait_recv()
             deliver_copies[half, q] = []
-            for step in (1, 3, 2, 0):
+            for step in (2, 1, 3, 0):
                 to = shifted(c, step)
 
-                def pack(j, carry, half=half, step=step, to=to):
-                    pages = gathered[half][q][source_table[(half * SIDE + to) * KIDS + j]]
-                    if step == 0:
-                        arrived[half, q, to, ALIVE + j] = pages
-                    else:
-                        outgoing[half, q, step - 1, j] = pages
+                def pack(batch, carry, half=half, step=step, to=to):
+                    slots = [batch * BATCH + i for i in range(BATCH)]
+                    sources = [source_table[(half * SIDE + to) * KIDS + j] for j in slots]
+                    blocks = [gathered[half][q][source] for source in sources]
+                    for j, block in zip(slots, blocks):
+                        if step == 0:
+                            arrived[half, q, to, ALIVE + j] = block
+                        else:
+                            outgoing[half, q, step - 1, j] = block
                     return carry
 
-                lax.fori_loop(0, KIDS, pack, 0)
+                lax.fori_loop(0, KIDS // BATCH, pack, 0)
                 if step:
                     copy = remote(
                         half, q, 6 + step, outgoing.at[half, q, step - 1],
@@ -332,11 +340,10 @@
             arrived, slot_queries, scores, terms, mixes, peak, mass, mixed, q, first, count)
 
     small_copies[0].wait()
-    lax.fori_loop(0, GROUPS, rank_group, 0)
-    small_copies[1].wait()
-    find_sources()
+    rank_group(group, 0)
     small_copies[2].wait()
-    pool_copy.wait()
+    for copy in pool_copies:
+        copy.wait()
     pack_alive(0)
     pl.semaphore_wait(barrier, 2 * (SIDE - 1) + MP - 1)
     spread(0)
@@ -345,6 +352,9 @@
         spread(q)
     send_features()
     load_weights()
+    small_copies[1].wait()
+    lax.fori_loop(0, GROUPS, rank_group, 0)
+    find_sources()
     for q in range(NQ):
         gather(q)
     invert_table()
@@ -356,14 +366,17 @@
     start_attention()
     for q in range(NQ):
         attend(q, 0, ALIVE)
-    for q in range(NQ):
+    late = [copy for half in range(2) for copy in deliver_copies[half, NQ - 1]]
+    for q in range(NQ - 1):
         for half in range(2):
             for copy in deliver_copies[half, q]:
                 copy.wait_recv()
-        if q < NQ - 1:
-            attend(q, ALIVE, KIDS)
+        attend(q, ALIVE, KIDS)
     for copy in started + feature_copies:
-        copy.wait_send()
+        if all(copy is not other for other in late):
+            copy.wait_send()
+    for copy in late:
+        copy.wait()
 
 
 def refill_kernel(
@@ -374,12 +387,16 @@
     pages = arrived.reshape(2 * NQ * SIDE * SLOTS * PQ, PAGE, 2 * HD)
     stores = []
     for part in range(RANGES):
-        def place(i, carry, part=part):
-            refilled[part * 128 + i] = pages[places_ref[part, i]]
+        def place(batch, carry, part=part):
+            at = [batch * 8 + i for i in range(8)]
+            places = [places_ref[part // 2, part % 2 * 64 + i] for i in at]
+            blocks = [pages[place] for place in places]
+            for i, block in zip(at, blocks):
+                refilled[part * 64 + i] = block
             return carry
 
-        lax.fori_loop(0, 128, place, 0, unroll=8)
-        some = pl.ds(part * 128, 128)
+        lax.fori_loop(0, 8, place, 0)
+        some = pl.ds(part * 64, 64)
         copy = pltpu.make_async_copy(refilled.at[some], refilled_ref.at[some], store_sem.at[part])
         copy.start()
         stores.append(copy)
@@ -454,7 +471,7 @@
             pltpu.SemaphoreType.DMA((2, NQ, 10)),
             pltpu.SemaphoreType.DMA((MP - 1,)),
             pltpu.SemaphoreType.DMA((MP - 1,)),
-            pltpu.SemaphoreType.DMA,
+            pltpu.SemaphoreType.DMA((RANGES,)),
             pltpu.SemaphoreType.DMA((MP, 3)),
             pltpu.SemaphoreType.DMA((6,)),
         ],

time: 81.3 us -> 79.1 us (0.973)
  Pallas kernels: 80.5 us -> 78.4 us
    pallas_call x1, Pallas kernels: 75.3 us -> 73.5 us  [shards(): pl.pallas_call(relay_kernel, out_shape=(pltpu.VMEM((2, NQ, SIDE, SLOTS, P...]
where the time goes in v3:
time: 79.1 us; the launch traced here: 79 us
  Pallas kernels  78.4 us (99%)
    pallas_call x1, Pallas kernels, shards(): pl.pallas_call(relay_kernel, out_shape=(pltpu.VMEM((2, NQ, SIDE, SLOTS, P...  73.5 us
    pallas_call x1, Pallas kernels, shards(): pl.pallas_call(refill_kernel, out_shape=(jax.ShapeDtypeStruct(pool.shape,...  4.91 us

profile of v3, /device:TPU:1, one launch (start us, length us, event | category | flops | bytes accessed | tf_op | source)
XLA Modules:
  0.0 79.0 jit_solution(14204296576797353762)
XLA Ops:
  0.6 73.5 %relay_pages_and_attend.1 = (bf16[2,3,4,18,2,16,256]{6,5,4,3,2,1,0:T(8,128)(2,1)S(1)}, f32[144,128]{1,0:T(8,128)S(1)}, f32[144,128]{1,0:T(8,128)S(1)}, f32[144,1...) custom-call(bf16[16,640]{1,0:T(8,128)(2,1)} %hidden_ref.1, f32[1,128]{1,0:T(1,128)} %bitcast.9, ...), custom_call_target="tpu_custom_call" | custom-call | tf_op jit(solution)/shard_map/relay_pages_and_attend/pallas_call | solution.py:438
  74.1 4.9 %refill_pool.1 = (bf16[768,16,256]{2,1,0:T(8,128)(2,1)}, bf16[16,1024]{1,0:T(8,128)(2,1)}) custom-call(bf16[2,3,4,18,2,16,256]{6,5,4,3,2,1,0:T(8,128)(2,1)S(1)} %get-tuple-element.10.arrived, f32[144,128]{1,0:T(8,128)S(1)} %get-tuple-element.11.slot_queries, f32[144,128]{1,0:T(8,128)S(1)} %get-tuple-element.12.peak, f32[144,128]{1,0:T(8,128)S(1)} %get-tuple-element.13.mass, ...), custom_call_target="tpu_custom_call" | custom-call | tf_op jit(solution)/shard_map/refill_pool/pallas_call | solution.py:482

commit v4 on v3

--- a/solution.py
+++ b/solution.py
@@ -65,10 +65,10 @@
     scratch = list(scratch)
     gathered = [[scratch.pop(0) for _ in range(NQ)] for _ in range(2)]
     (outgoing, pool, features, w_query, w_key, w_value, project, queries, keys, values,
-     scores, terms, mixes,
+     scores, terms, mixes, places,
      query_gain_ref, key_gain_ref, table_ref, parent_ref, surviving_ref,
      alive_table, rank_table, source_table, child_table, slot_table,
-     send_sem, recv_sem, feature_send, feature_recv, pool_sem, weight_sem, small_sem) = scratch
+     send_sem, recv_sem, feature_send, feature_recv, pool_sem, weight_sem, small_sem, places_sem) = scratch
 
     group = lax.axis_index("dp")
     part = lax.axis_index("mp")
@@ -88,6 +88,13 @@
         pltpu.make_async_copy(pool_ref.at[pl.ds(i * 64, 64)], pool.at[pl.ds(i * 64, 64)], pool_sem.at[i])
         for i in range(RANGES)
     ]
+    barrier = pltpu.get_barrier_semaphore()
+    for step in range(1, SIDE):
+        pl.semaphore_signal(barrier, inc=1, device_id=device(0, z, shifted(y, step)), device_id_type=MESH)
+        pl.semaphore_signal(barrier, inc=1, device_id=device(1, y, shifted(z, step)), device_id_type=MESH)
+    for step in range(1, MP):
+        pl.semaphore_signal(barrier, inc=1, device_id=(group, shifted(part, step, MP)), device_id_type=MESH)
+
     small_copies = [
         pltpu.make_async_copy(source, target, small_sem.at[i])
         for i, (source, target) in enumerate((
@@ -99,13 +106,6 @@
         copy.start()
     for copy in pool_copies:
         copy.start()
-
-    barrier = pltpu.get_barrier_semaphore()
-    for step in range(1, SIDE):
-        pl.semaphore_signal(barrier, inc=1, device_id=device(0, z, shifted(y, step)), device_id_type=MESH)
-        pl.semaphore_signal(barrier, inc=1, device_id=device(1, y, shifted(z, step)), device_id_type=MESH)
-    for step in range(1, MP):
-        pl.semaphore_signal(barrier, inc=1, device_id=(group, shifted(part, step, MP)), device_id_type=MESH)
 
     def rank_group(at, carry):
         found = [jnp.int32(99) for _ in range(ALIVE)]
@@ -161,19 +161,22 @@
         lane = lax.broadcasted_iota(jnp.int32, (8, 128), 1)
         page_ids = row * 128 + lane
 
-        def one_branch(b, places):
+        def one_branch(b, found):
             slot = slot_table[b]
-            places = jnp.where((row == 7) & (lane == b), slot, places)
+            found = jnp.where((row == 7) & (lane == b), slot, found)
             for half in range(2):
                 for c in range(SIDE):
                     for q in range(NQ):
                         for r in range(PQ):
                             page = table_ref[half * HALF + c * PIECE + q * PQ + r, group * BR + b]
                             place = (((half * NQ + q) * SIDE + c) * SLOTS + slot) * PQ + r
-                            places = jnp.where(page_ids == page, place, places)
-            return places
-
-        places_ref[...] = lax.fori_loop(0, BR, one_branch, jnp.zeros((8, 128), jnp.int32))
+                            found = jnp.where(page_ids == page, place, found)
+            return found
+
+        places[...] = lax.fori_loop(0, BR, one_branch, jnp.zeros((8, 128), jnp.int32))
+        copy = pltpu.make_async_copy(places, places_ref, places_sem)
+        copy.start()
+        copy.wait()
 
     feature_copies, weight_copies = [], []
     rows = hidden_ref.shape[1]
@@ -357,11 +360,11 @@
     find_sources()
     for q in range(NQ):
         gather(q)
-    invert_table()
     for q in range(NQ):
         forward(q)
     for q in range(NQ):
         deliver(q)
+    invert_table()
     project_tokens()
     start_attention()
     for q in range(NQ):
@@ -440,10 +443,10 @@
         out_shape=(
             pltpu.VMEM((2, NQ, SIDE, SLOTS, PQ) + page_shape, bf16),
             state, state, state, state,
-            jax.ShapeDtypeStruct((8, 128), i32),
+            pltpu.SMEM((8, 128), i32),
         ),
         in_specs=[hbm] * 10,
-        out_specs=(vmem,) * 6,
+        out_specs=(vmem,) * 5 + (smem,),
         scratch_shapes=[pltpu.VMEM((GROUPS * ALIVE, PQ) + page_shape, bf16)] * (2 * NQ)
         + [
             pltpu.VMEM((2, NQ, SIDE - 1, KIDS, PQ) + page_shape, bf16),
@@ -457,6 +460,7 @@
             pltpu.VMEM((BR, 1, HD), f32),
             pltpu.VMEM((BR, 1, HD), f32),
             *chunk,
+            pltpu.VMEM((8, 128), i32),
             pltpu.VMEM((1, HD), f32),
             pltpu.VMEM((1, HD), f32),
             pltpu.SMEM(table.shape, i32),
@@ -474,6 +478,7 @@
             pltpu.SemaphoreType.DMA((RANGES,)),
             pltpu.SemaphoreType.DMA((MP, 3)),
             pltpu.SemaphoreType.DMA((6,)),
+            pltpu.SemaphoreType.DMA,
         ],
         compiler_params=pltpu.CompilerParams(
             collective_id=0, has_side_effects=True, vmem_limit_bytes=44 * 2**20),

time: 79.1 us -> 78.4 us (level)
  no operation moved by 1% of the time
where the time goes in v4:
time: 78.4 us; the launch traced here: 78.3 us
  Pallas kernels  77.7 us (99%)
    pallas_call x1, Pallas kernels, shards(): pl.pallas_call(relay_kernel, out_shape=(pltpu.VMEM((2, NQ, SIDE, SLOTS, P...  73.5 us
    pallas_call x1, Pallas kernels, shards(): pl.pallas_call(refill_kernel, out_shape=(jax.ShapeDtypeStruct(pool.shape,...  4.23 us

profile of v4, /device:TPU:1, one launch (start us, length us, event | category | flops | bytes accessed | tf_op | source)
XLA Modules:
  0.0 78.3 jit_solution(3105858271667064945)
XLA Ops:
  0.6 73.5 %relay_pages_and_attend.1 = (bf16[2,3,4,18,2,16,256]{6,5,4,3,2,1,0:T(8,128)(2,1)S(1)}, f32[144,128]{1,0:T(8,128)S(1)}, f32[144,128]{1,0:T(8,128)S(1)}, f32[144,1...) custom-call(bf16[16,640]{1,0:T(8,128)(2,1)} %hidden_ref.1, f32[1,128]{1,0:T(1,128)} %bitcast.9, ...), custom_call_target="tpu_custom_call" | custom-call | tf_op jit(solution)/shard_map/relay_pages_and_attend/pallas_call | solution.py:441
  74.1 4.2 %refill_pool.1 = (bf16[768,16,256]{2,1,0:T(8,128)(2,1)}, bf16[16,1024]{1,0:T(8,128)(2,1)}) custom-call(bf16[2,3,4,18,2,16,256]{6,5,4,3,2,1,0:T(8,128)(2,1)S(1)} %get-tuple-element.10.arrived, f32[144,128]{1,0:T(8,128)S(1)} %get-tuple-element.11.slot_queries, f32[144,128]{1,0:T(8,128)S(1)} %get-tuple-element.12.peak, f32[144,128]{1,0:T(8,128)S(1)} %get-tuple-element.13.mass, ...), custom_call_target="tpu_custom_call" | custom-call | tf_op jit(solution)/shard_map/refill_pool/pallas_call | solution.py:487

commit v5 on v4

--- a/solution.py
+++ b/solution.py
@@ -84,16 +84,19 @@
     def shifted(value, step, size=SIDE):
         return (value + step + size) % size
 
-    pool_copies = [
-        pltpu.make_async_copy(pool_ref.at[pl.ds(i * 64, 64)], pool.at[pl.ds(i * 64, 64)], pool_sem.at[i])
-        for i in range(RANGES)
-    ]
+    pool_copy = pltpu.make_async_copy(pool_ref, pool, pool_sem)
     barrier = pltpu.get_barrier_semaphore()
-    for step in range(1, SIDE):
+    def greet_line(step, carry):
         pl.semaphore_signal(barrier, inc=1, device_id=device(0, z, shifted(y, step)), device_id_type=MESH)
         pl.semaphore_signal(barrier, inc=1, device_id=device(1, y, shifted(z, step)), device_id_type=MESH)
-    for step in range(1, MP):
+        return carry
+
+    def greet_part(step, carry):
         pl.semaphore_signal(barrier, inc=1, device_id=(group, shifted(part, step, MP)), device_id_type=MESH)
+        return carry
+
+    lax.fori_loop(1, SIDE, greet_line, 0)
+    lax.fori_loop(1, MP, greet_part, 0)
 
     small_copies = [
         pltpu.make_async_copy(source, target, small_sem.at[i])
@@ -104,8 +107,7 @@
     ]
     for copy in small_copies:
         copy.start()
-    for copy in pool_copies:
-        copy.start()
+    pool_copy.start()
 
     def rank_group(at, carry):
         found = [jnp.int32(99) for _ in range(ALIVE)]
@@ -345,8 +347,7 @@
     small_copies[0].wait()
     rank_group(group, 0)
     small_copies[2].wait()
-    for copy in pool_copies:
-        copy.wait()
+    pool_copy.wait()
     pack_alive(0)
     pl.semaphore_wait(barrier, 2 * (SIDE - 1) + MP - 1)
     spread(0)
@@ -388,21 +389,24 @@
     refilled, scores, terms, mixes, final, result, store_sem,
 ):
     pages = arrived.reshape(2 * NQ * SIDE * SLOTS * PQ, PAGE, 2 * HD)
-    stores = []
-    for part in range(RANGES):
-        def place(batch, carry, part=part):
-            at = [batch * 8 + i for i in range(8)]
+    stores = [
+        pltpu.make_async_copy(
+            refilled.at[pl.ds(part * 64, 64)], refilled_ref.at[pl.ds(part * 64, 64)], store_sem.at[part])
+        for part in range(RANGES)
+    ]
+
+    def place(part, carry):
+        for batch in range(4):
+            at = [batch * 16 + i for i in range(16)]
             places = [places_ref[part // 2, part % 2 * 64 + i] for i in at]
             blocks = [pages[place] for place in places]
             for i, block in zip(at, blocks):
                 refilled[part * 64 + i] = block
-            return carry
-
-        lax.fori_loop(0, 8, place, 0)
         some = pl.ds(part * 64, 64)
-        copy = pltpu.make_async_copy(refilled.at[some], refilled_ref.at[some], store_sem.at[part])
-        copy.start()
-        stores.append(copy)
+        pltpu.make_async_copy(refilled.at[some], refilled_ref.at[some], store_sem.at[part]).start()
+        return carry
+
+    lax.fori_loop(0, RANGES, place, 0)
     alive = pl.ds(0, ALIVE * HEADS)
     final[alive] = mixed[alive] / mass[alive]
     _, total, mix = attend_chunk(
@@ -475,7 +479,7 @@
             pltpu.SemaphoreType.DMA((2, NQ, 10)),
             pltpu.SemaphoreType.DMA((MP - 1,)),
             pltpu.SemaphoreType.DMA((MP - 1,)),
-            pltpu.SemaphoreType.DMA((RANGES,)),
+            pltpu.SemaphoreType.DMA,
             pltpu.SemaphoreType.DMA((MP, 3)),
             pltpu.SemaphoreType.DMA((6,)),
             pltpu.SemaphoreType.DMA,

time: 78.4 us -> 77.7 us (level)
  Pallas kernels: 77.7 us -> 76.9 us
where the time goes in v5:
time: 77.7 us; the launch traced here: 77.6 us
  Pallas kernels  76.9 us (99%)
    pallas_call x1, Pallas kernels, shards(): pl.pallas_call(relay_kernel, out_shape=(pltpu.VMEM((2, NQ, SIDE, SLOTS, P...  73.4 us
    pallas_call x1, Pallas kernels, shards(): pl.pallas_call(refill_kernel, out_shape=(jax.ShapeDtypeStruct(pool.shape,...  3.53 us

profile of v5, /device:TPU:1, one launch (start us, length us, event | category | flops | bytes accessed | tf_op | source)
XLA Modules:
  0.0 77.6 jit_solution(13838439961259262557)
XLA Ops:
  0.6 73.4 %relay_pages_and_attend.1 = (bf16[2,3,4,18,2,16,256]{6,5,4,3,2,1,0:T(8,128)(2,1)S(1)}, f32[144,128]{1,0:T(8,128)S(1)}, f32[144,128]{1,0:T(8,128)S(1)}, f32[144,1...) custom-call(bf16[16,640]{1,0:T(8,128)(2,1)} %hidden_ref.1, f32[1,128]{1,0:T(1,128)} %bitcast.9, ...), custom_call_target="tpu_custom_call" | custom-call | tf_op jit(solution)/shard_map/relay_pages_and_attend/pallas_call | solution.py:445
  74.0 3.5 %refill_pool.1 = (bf16[768,16,256]{2,1,0:T(8,128)(2,1)}, bf16[16,1024]{1,0:T(8,128)(2,1)}) custom-call(bf16[2,3,4,18,2,16,256]{6,5,4,3,2,1,0:T(8,128)(2,1)S(1)} %get-tuple-element.10.arrived, f32[144,128]{1,0:T(8,128)S(1)} %get-tuple-element.11.slot_queries, f32[144,128]{1,0:T(8,128)S(1)} %get-tuple-element.12.peak, f32[144,128]{1,0:T(8,128)S(1)} %get-tuple-element.13.mass, ...), custom_call_target="tpu_custom_call" | custom-call | tf_op jit(solution)/shard_map/refill_pool/pallas_call | solution.py:491

commit v6 on v5

--- a/solution.py
+++ b/solution.py
@@ -17,8 +17,8 @@
 ALIVE = 4
 KIDS = 14
 SIDE = 4
-NQ = 3
-PQ = 2
+NQ = 2
+PQ = 3
 PIECE = NQ * PQ
 HALF = NPAGE // 2
 MP = 8
@@ -63,7 +63,7 @@
     *scratch,
 ):
     scratch = list(scratch)
-    gathered = [[scratch.pop(0) for _ in range(NQ)] for _ in range(2)]
+    gathered = [scratch.pop(0) for _ in range(NQ)]
     (outgoing, pool, features, w_query, w_key, w_value, project, queries, keys, values,
      scores, terms, mixes, places,
      query_gain_ref, key_gain_ref, table_ref, parent_ref, surviving_ref,
@@ -73,8 +73,6 @@
     group = lax.axis_index("dp")
     part = lax.axis_index("mp")
     z, y = group // SIDE, group % SIDE
-    along = [z, y]
-    across = [y, z]
 
     def device(half, gather_at, spread_at):
         if half == 0:
@@ -139,7 +137,7 @@
                     rank = rank_table[parent]
                     if half == 1:
                         from_group = (from_group % SIDE) * SIDE + from_group // SIDE
-                    source_table[(half * SIDE + spread_at) * KIDS + j] = from_group * ALIVE + rank
+                    source_table[(half * SIDE + spread_at) * KIDS + j] = (half * GROUPS + from_group) * ALIVE + rank
                     return carry
 
                 lax.fori_loop(0, KIDS, find_source, 0)
@@ -205,13 +203,28 @@
             weight_copies.append(copies)
 
     def remote(half, q, kind, source, target, gather_at, spread_at):
+        to = jnp.where(half == 0, gather_at * SIDE + spread_at, spread_at * SIDE + gather_at)
         return pltpu.make_async_remote_copy(
             src_ref=source, dst_ref=target,
             send_sem=send_sem.at[half, q, kind], recv_sem=recv_sem.at[half, q, kind],
-            device_id=device(half, gather_at, spread_at), device_id_type=MESH)
-
-    spread_copies, gather_copies, forward_copies, deliver_copies = {}, {}, {}, {}
-    started = []
+            device_id=(to, part), device_id_type=MESH)
+
+    def place_of(half):
+        return jnp.where(half == 0, z, y), jnp.where(half == 0, y, z)
+
+    def each_half(body):
+        def run(half, carry):
+            body(half, *place_of(half))
+            return carry
+
+        lax.fori_loop(0, 2, run, 0)
+
+    def each_step(first, last, body):
+        def run(step, carry):
+            body(step)
+            return carry
+
+        lax.fori_loop(first, last, run, 0)
 
     def pack_alive(q):
         def one(k, carry):
@@ -226,77 +239,93 @@
 
         lax.fori_loop(0, ALIVE, one, 0)
 
+    def spread_copy(q, half, a, c, step):
+        to = shifted(c, step)
+        here = pl.ds(half * 64 + a * 16 + c * 4, 4)
+        return remote(
+            half, q, step - 1, arrived.at[half, q, to, pl.ds(0, ALIVE)], gathered[q].at[here], a, to)
+
     def spread(q):
-        for half in range(2):
-            a, c = along[half], across[half]
-            here = pl.ds(a * 16 + c * 4, 4)
-            copies = []
-            for step in (2, 1, 3):
-                to = shifted(c, step)
-                copy = remote(
-                    half, q, step - 1, arrived.at[half, q, to, pl.ds(0, ALIVE)], gathered[half][q].at[here], a, to)
-                copy.start()
-                copies.append(copy)
-            gathered[half][q][here] = arrived[half, q, c, 0:ALIVE]
-            spread_copies[half, q] = copies
-            started.extend(copies)
+        def one(half, a, c):
+            each_step(1, SIDE, lambda step: spread_copy(q, half, a, c, step).start())
+            gathered[q][pl.ds(half * 64 + a * 16 + c * 4, 4)] = arrived[half, q, c, 0:ALIVE]
+
+        each_half(one)
+
+    def gather_copy(q, half, a, c, way):
+        block = gathered[q].at[pl.ds(half * 64 + a * 16, 16)]
+        return remote(half, q, 3 + way, block, block, shifted(a, 1 - 2 * way), c)
 
     def gather(q):
-        for half in range(2):
-            a, c = along[half], across[half]
-            for copy in spread_copies[half, q]:
-                copy.wait_recv()
-            block = gathered[half][q].at[pl.ds(a * 16, 16)]
-            copies = []
-            for kind, step in ((3, 1), (4, -1)):
-                copy = remote(half, q, kind, block, block, shifted(a, step), c)
-                copy.start()
-                copies.append(copy)
-            gather_copies[half, q] = copies
-            started.extend(copies)
+        def one(half, a, c):
+            each_step(1, SIDE, lambda step: spread_copy(q, half, a, c, step).wait_recv())
+            each_step(0, 2, lambda way: gather_copy(q, half, a, c, way).start())
+
+        each_half(one)
+
+    def forward_copy(q, half, a, c, way):
+        step = 1 - 2 * way
+        block = gathered[q].at[pl.ds(half * 64 + shifted(a, -step) * 16 + way * 8, 8)]
+        return remote(half, q, 5 + way, block, block, shifted(a, step), c)
 
     def forward(q):
-        for half in range(2):
-            a, c = along[half], across[half]
-            for copy in gather_copies[half, q]:
-                copy.wait_recv()
-            copies = []
-            for kind, step, first in ((5, 1, 0), (6, -1, 8)):
-                block = gathered[half][q].at[pl.ds(shifted(a, -step) * 16 + first, 8)]
-                copy = remote(half, q, kind, block, block, shifted(a, step), c)
-                copy.start()
-                copies.append(copy)
-            forward_copies[half, q] = copies
-            started.extend(copies)
+        def one(half, a, c):
+            each_step(0, 2, lambda way: gather_copy(q, half, a, c, way).wait_recv())
+            each_step(0, 2, lambda way: forward_copy(q, half, a, c, way).start())
+
+        each_half(one)
+
+    def deliver_copy(q, half, a, c, step):
+        return remote(
+            half, q, 6 + step, outgoing.at[half, q, step - 1],
+            arrived.at[half, q, c, pl.ds(ALIVE, KIDS)], a, shifted(c, step))
 
     def deliver(q):
-        for half in range(2):
-            a, c = along[half], across[half]
-            for copy in forward_copies[half, q]:
-                copy.wait_recv()
-            deliver_copies[half, q] = []
-            for step in (2, 1, 3, 0):
-                to = shifted(c, step)
-
-                def pack(batch, carry, half=half, step=step, to=to):
+        each_half(lambda half, a, c: each_step(
+            0, 2, lambda way: forward_copy(q, half, a, c, way).wait_recv()))
+
+        def one(half, a, c):
+            def pack(to, put):
+                def few(batch, carry):
                     slots = [batch * BATCH + i for i in range(BATCH)]
                     sources = [source_table[(half * SIDE + to) * KIDS + j] for j in slots]
-                    blocks = [gathered[half][q][source] for source in sources]
+                    blocks = [gathered[q][source] for source in sources]
                     for j, block in zip(slots, blocks):
-                        if step == 0:
-                            arrived[half, q, to, ALIVE + j] = block
-                        else:
-                            outgoing[half, q, step - 1, j] = block
+                        put(j, block)
                     return carry
 
-                lax.fori_loop(0, KIDS // BATCH, pack, 0)
-                if step:
-                    copy = remote(
-                        half, q, 6 + step, outgoing.at[half, q, step - 1],
-                        arrived.at[half, q, c, pl.ds(ALIVE, KIDS)], a, to)
-                    copy.start()
-                    deliver_copies[half, q].append(copy)
-                    started.append(copy)
+                lax.fori_loop(0, KIDS // BATCH, few, 0)
+
+            def send(step):
+                def put(j, block):
+                    outgoing[half, q, step - 1, j] = block
+
+                pack(shifted(c, step), put)
+                deliver_copy(q, half, a, c, step).start()
+
+            def keep(j, block):
+                arrived[half, q, c, ALIVE + j] = block
+
+            each_step(1, SIDE, send)
+            pack(c, keep)
+
+        each_half(one)
+
+    def wait_delivered(q):
+        each_half(lambda half, a, c: each_step(
+            1, SIDE, lambda step: deliver_copy(q, half, a, c, step).wait_recv()))
+
+    def wait_sent(q):
+        def one(half, a, c):
+            each_step(1, SIDE, lambda step: spread_copy(q, half, a, c, step).wait_send())
+            each_step(0, 2, lambda way: gather_copy(q, half, a, c, way).wait_send())
+            each_step(0, 2, lambda way: forward_copy(q, half, a, c, way).wait_send())
+
+        each_half(one)
+
+    def wait_delivery_sent(q):
+        each_half(lambda half, a, c: each_step(
+            1, SIDE, lambda step: deliver_copy(q, half, a, c, step).wait_send()))
 
     def normalize(block, gain):
         return block * lax.rsqrt(jnp.mean(block * block, -1, keepdims=True) + 1e-06) * gain
@@ -370,17 +399,17 @@
     start_attention()
     for q in range(NQ):
         attend(q, 0, ALIVE)
-    late = [copy for half in range(2) for copy in deliver_copies[half, NQ - 1]]
     for q in range(NQ - 1):
-        for half in range(2):
-            for copy in deliver_copies[half, q]:
-                copy.wait_recv()
+        wait_delivered(q)
         attend(q, ALIVE, KIDS)
-    for copy in started + feature_copies:
-        if all(copy is not other for other in late):
-            copy.wait_send()
-    for copy in late:
-        copy.wait()
+    for q in range(NQ):
+        wait_sent(q)
+        if q < NQ - 1:
+            wait_delivery_sent(q)
+    for copy in feature_copies:
+        copy.wait_send()
+    wait_delivered(NQ - 1)
+    wait_delivery_sent(NQ - 1)
 
 
 def refill_kernel(
@@ -451,7 +480,7 @@
         ),
         in_specs=[hbm] * 10,
         out_specs=(vmem,) * 5 + (smem,),
-        scratch_shapes=[pltpu.VMEM((GROUPS * ALIVE, PQ) + page_shape, bf16)] * (2 * NQ)
+        scratch_shapes=[pltpu.VMEM((2 * GROUPS * ALIVE, PQ) + page_shape, bf16)] * NQ
         + [
             pltpu.VMEM((2, NQ, SIDE - 1, KIDS, PQ) + page_shape, bf16),
             pltpu.VMEM(pool.shape, bf16),

time: 77.7 us -> 77.2 us (level)
  no operation moved by 1% of the time
where the time goes in v6:
time: 77.2 us; the launch traced here: 77 us
  Pallas kernels  76.4 us (99%)
    pallas_call x1, Pallas kernels, shards(): pl.pallas_call(relay_kernel, out_shape=(pltpu.VMEM((2, NQ, SIDE, SLOTS, P...  72.7 us
    pallas_call x1, Pallas kernels, shards(): pl.pallas_call(refill_kernel, out_shape=(jax.ShapeDtypeStruct(pool.shape,...  3.66 us

profile of v6, /device:TPU:1, one launch (start us, length us, event | category | flops | bytes accessed | tf_op | source)
XLA Modules:
  0.0 77.0 jit_solution(2294956627323131445)
XLA Ops:
  0.6 72.7 %relay_pages_and_attend.1 = (bf16[2,2,4,18,3,16,256]{6,5,4,3,2,1,0:T(8,128)(2,1)S(1)}, f32[144,128]{1,0:T(8,128)S(1)}, f32[144,128]{1,0:T(8,128)S(1)}, f32[144,1...) custom-call(bf16[16,640]{1,0:T(8,128)(2,1)} %hidden_ref.1, f32[1,128]{1,0:T(1,128)} %bitcast.9, ...), custom_call_target="tpu_custom_call" | custom-call | tf_op jit(solution)/shard_map/relay_pages_and_attend/pallas_call | solution.py:474
  73.4 3.7 %refill_pool.1 = (bf16[768,16,256]{2,1,0:T(8,128)(2,1)}, bf16[16,1024]{1,0:T(8,128)(2,1)}) custom-call(bf16[2,2,4,18,3,16,256]{6,5,4,3,2,1,0:T(8,128)(2,1)S(1)} %get-tuple-element.10.arrived, f32[144,128]{1,0:T(8,128)S(1)} %get-tuple-element.11.slot_queries, f32[144,128]{1,0:T(8,128)S(1)} %get-tuple-element.12.peak, f32[144,128]{1,0:T(8,128)S(1)} %get-tuple-element.13.mass, ...), custom_call_target="tpu_custom_call" | custom-call | tf_op jit(solution)/shard_map/refill_pool/pallas_call | solution.py:520

commit v7 on v6

--- a/solution.py
+++ b/solution.py
@@ -399,6 +399,8 @@
     start_attention()
     for q in range(NQ):
         attend(q, 0, ALIVE)
+    done = pl.ds(0, ALIVE * HEADS)
+    mixed[done] = mixed[done] / mass[done]
     for q in range(NQ - 1):
         wait_delivered(q)
         attend(q, ALIVE, KIDS)
@@ -437,7 +439,7 @@
 
     lax.fori_loop(0, RANGES, place, 0)
     alive = pl.ds(0, ALIVE * HEADS)
-    final[alive] = mixed[alive] / mass[alive]
+    final[alive] = mixed[alive]
     _, total, mix = attend_chunk(
         arrived, slot_queries, scores, terms, mixes, peak, mass, mixed, NQ - 1, ALIVE, KIDS)
     final[pl.ds(ALIVE * HEADS, KIDS * HEADS)] = mix / total

time: 77.2 us -> 77.2 us (level)
  no operation moved by 1% of the time
where the time goes in v7:
time: 77.2 us; the launch traced here: 77 us
  Pallas kernels  76.4 us (99%)
    pallas_call x1, Pallas kernels, shards(): pl.pallas_call(relay_kernel, out_shape=(pltpu.VMEM((2, NQ, SIDE, SLOTS, P...  72.7 us
    pallas_call x1, Pallas kernels, shards(): pl.pallas_call(refill_kernel, out_shape=(jax.ShapeDtypeStruct(pool.shape,...  3.66 us

profile of v7, /device:TPU:1, one launch (start us, length us, event | category | flops | bytes accessed | tf_op | source)
XLA Modules:
  0.0 77.0 jit_solution(12176570932946351897)
XLA Ops:
  0.6 72.7 %relay_pages_and_attend.1 = (bf16[2,2,4,18,3,16,256]{6,5,4,3,2,1,0:T(8,128)(2,1)S(1)}, f32[144,128]{1,0:T(8,128)S(1)}, f32[144,128]{1,0:T(8,128)S(1)}, f32[144,1...) custom-call(bf16[16,640]{1,0:T(8,128)(2,1)} %hidden_ref.1, f32[1,128]{1,0:T(1,128)} %bitcast.9, ...), custom_call_target="tpu_custom_call" | custom-call | tf_op jit(solution)/shard_map/relay_pages_and_attend/pallas_call | solution.py:476
  73.4 3.7 %refill_pool.1 = (bf16[768,16,256]{2,1,0:T(8,128)(2,1)}, bf16[16,1024]{1,0:T(8,128)(2,1)}) custom-call(bf16[2,2,4,18,3,16,256]{6,5,4,3,2,1,0:T(8,128)(2,1)S(1)} %get-tuple-element.10.arrived, f32[144,128]{1,0:T(8,128)S(1)} %get-tuple-element.11.slot_queries, f32[144,128]{1,0:T(8,128)S(1)} %get-tuple-element.12.peak, f32[144,128]{1,0:T(8,128)S(1)} %get-tuple-element.13.mass, ...), custom_call_target="tpu_custom_call" | custom-call | tf_op jit(solution)/shard_map/refill_pool/pallas_call | solution.py:522
